TPU v7x, 256 devices: a whole 4x4x8 slice. The times are simulated.
256 devices in a mesh: context: 64 (over x, y_lo, z), dp: 4 (over y_hi, core).
Axes of the slice: x: 4, y: 4 (y_hi: 2, y_lo: 2; y = y_hi * 2 + y_lo), z: 8, core: 2. Of those that a mesh axis runs over, the one named last changes fastest.
Arguments:
- queries: bfloat16 [4, 8192, 1024], P('dp', 'context'), may hold values from -12 to 12
- key_states: bfloat16 [4, 8192, 128], P('dp', 'context'), may hold values from -12 to 12
- value_states: bfloat16 [4, 8192, 128], P('dp', 'context'), may hold values from -6 to 6
- attn_out: bfloat16 [4, 8192, 1024], P('dp', 'context'), may hold values from -6 to 6
- out_grad: bfloat16 [4, 8192, 1024], P('dp', 'context'), may hold values from -6 to 6
- activations: bfloat16 [4, 8192, 8192], P('dp', 'context'), may hold values from -6 to 6
- segment_ids: int32 [4, 8192], P('dp', 'context'), may hold values from 0 to 3, as said below
- span_order: int32 [128], replicated, may hold values from 0 to 127, as said below
- kv_weight: float32 [2, 8192, 128], P(None, ('context', 'dp')), may hold values from -40 to 40
- moment_one: float32 [2, 8192, 128], P(None, ('context', 'dp')), may hold values from -200 to 200
- moment_two: float32 [2, 8192, 128], P(None, ('context', 'dp')), may hold values from 2 to 20000
Outputs:
- query_grad: bfloat16 [4, 8192, 1024], P('dp', 'context')
- kv_grad: bfloat16 [4, 8192, 256], P('dp', 'context')
- new_weight: float32 [2, 8192, 128], P(None, ('context', 'dp'))
- new_moment_one: float32 [2, 8192, 128], P(None, ('context', 'dp'))
- new_moment_two: float32 [2, 8192, 128], P(None, ('context', 'dp'))
- trust_ratio: float32 [2], replicated
Inputs may be any that keep to these rules, and one draw needn't show every extreme that they name: `span_order`: stored spans 2i and 2i+1 hold the sequence's spans p and 127 - p, each span exactly once. `segment_ids`: along positions the ids never fall; every sequence holds ids 0 to 3; the document of the last position holds 8 positions or more.
All inputs are finite; a program needn't handle non-finite values.
Results may differ from a plain program's by a relative error of at most 0.0055.
Values may be sent and summed in bfloat16 or wider, within the bound.
A program may use at most 64 MiB of HBM per device.

v0:
```python
import jax
import jax.numpy as jnp
from jax import lax
from jax.sharding import PartitionSpec as P

beta_one = 0.9
beta_two = 0.999
epsilon = 1e-06
weight_decay = 0.01
learn_rate = 0.01


def layout_positions(span_order, first_row, row_count, half):
    layout = first_row + jnp.arange(row_count, dtype=jnp.int32)
    which = layout // half
    table = jnp.arange(span_order.shape[0], dtype=jnp.int32)
    picked = jnp.sum(jnp.where(which[:, None] == table[None, :], span_order[None, :], 0), axis=1)
    return picked * half + layout % half


def block_size(total_rows, query_rows):
    block_rows = total_rows
    while block_rows > 4 * query_rows and block_rows % 2 == 0:
        block_rows = block_rows // 2
    return block_rows


def on_device(
    queries,
    key_states,
    value_states,
    attn_out,
    out_grad,
    activations,
    segment_ids,
    span_order,
    kv_weight,
    moment_one,
    moment_two,
):
    device = lax.axis_index("context")
    query_rows = queries.shape[1]
    half = query_rows // 2
    head_dim = key_states.shape[2]
    heads = queries.shape[2] // head_dim
    score_scale = head_dim ** (-0.5)
    query_heads = queries[0].reshape(query_rows, heads, head_dim)
    grad_heads = out_grad[0].reshape(query_rows, heads, head_dim)
    output_heads = attn_out[0].reshape(query_rows, heads, head_dim)
    delta = jnp.sum(grad_heads.astype(jnp.float32) * output_heads.astype(jnp.float32), axis=2)
    query_place = layout_positions(span_order, device * query_rows, query_rows, half)
    query_segment = segment_ids[0]
    all_segments = lax.all_gather(segment_ids, "context", axis=1, tiled=True)[0]

    def visible_for(first_row, row_count):
        key_place = layout_positions(span_order, first_row, row_count, half)
        key_segment = lax.dynamic_slice_in_dim(all_segments, first_row, row_count, 0)
        visible = (key_place[None, :] <= query_place[:, None]) & (
            key_segment[None, :] == query_segment[:, None]
        )
        return visible[:, None, :]

    def score_block(key_block):
        return (
            jnp.einsum("qhd,kd->qhk", query_heads, key_block, preferred_element_type=jnp.float32)
            * score_scale
        )

    seq_length = query_rows * lax.axis_size("context")
    start_stats = (
        jnp.full((query_rows, heads), -1e30, jnp.float32),
        jnp.zeros((query_rows, heads), jnp.float32),
    )
    start_grads = (
        jnp.zeros((query_rows, heads, head_dim), jnp.float32),
        jnp.zeros((seq_length, 2 * head_dim), jnp.float32),
    )
    key_piece = lax.all_gather(key_states, "context", axis=1, tiled=True)
    piece_rows = key_piece.shape[1]
    block_rows = block_size(piece_rows, query_rows)

    def stats_step(block_index, state):
        row_top, row_total = state
        offset = block_index * block_rows
        key_block = lax.dynamic_slice_in_dim(key_piece[0], offset, block_rows, 0)
        visible = visible_for(offset, block_rows)
        scores = score_block(key_block)
        masked = jnp.where(visible, scores, -1e30)
        new_top = jnp.maximum(row_top, jnp.max(masked, axis=2))
        weights = jnp.where(visible, jnp.exp(scores - new_top[:, :, None]), 0.0)
        return (new_top, row_total * jnp.exp(row_top - new_top) + jnp.sum(weights, axis=2))

    row_top, row_total = lax.fori_loop(0, piece_rows // block_rows, stats_step, start_stats)
    log_total = row_top + jnp.log(row_total)
    fold_key_piece = lax.all_gather(key_states, "context", axis=1, tiled=True)
    value_piece = lax.all_gather(value_states, "context", axis=1, tiled=True)
    piece_rows = fold_key_piece.shape[1]
    fold_block_rows = block_size(piece_rows, query_rows)

    def grad_step(block_index, state):
        query_acc, kv_acc = state
        offset = block_index * fold_block_rows
        key_block = lax.dynamic_slice_in_dim(fold_key_piece[0], offset, fold_block_rows, 0)
        value_block = lax.dynamic_slice_in_dim(value_piece[0], offset, fold_block_rows, 0)
        visible = visible_for(offset, fold_block_rows)
        probs = jnp.where(visible, jnp.exp(score_block(key_block) - log_total[:, :, None]), 0.0)
        prob_grad = jnp.einsum(
            "qhd,kd->qhk", grad_heads, value_block, preferred_element_type=jnp.float32
        )
        score_grad = (score_scale * probs * (prob_grad - delta[:, :, None])).astype(jnp.bfloat16)
        query_acc = query_acc + jnp.einsum(
            "qhk,kd->qhd", score_grad, key_block, preferred_element_type=jnp.float32
        )
        key_grad = jnp.einsum(
            "qhk,qhd->kd", score_grad, query_heads, preferred_element_type=jnp.float32
        )
        value_grad = jnp.einsum(
            "qhk,qhd->kd",
            probs.astype(jnp.bfloat16),
            grad_heads,
            preferred_element_type=jnp.float32,
        )
        current = lax.dynamic_slice_in_dim(kv_acc, offset, fold_block_rows, 0)
        summed = current + jnp.concatenate([key_grad, value_grad], axis=1)
        return (query_acc, lax.dynamic_update_slice_in_dim(kv_acc, summed, offset, 0))

    query_acc, kv_acc = lax.fori_loop(0, piece_rows // fold_block_rows, grad_step, start_grads)
    kv_summed = lax.psum_scatter(kv_acc, "context", scatter_dimension=0, tiled=True)
    kv_low = kv_summed.astype(jnp.bfloat16)
    feature_rows = activations[0]
    gradient = lax.psum_scatter(
        lax.dot_general(
            feature_rows, kv_low, (((0,), (0,)), ((), ())), preferred_element_type=jnp.float32
        ),
        ("context", "dp"),
        scatter_dimension=0,
        tiled=True,
    )
    gradient = jnp.stack([gradient[:, :head_dim], gradient[:, head_dim:]])
    new_one = beta_one * moment_one + (1.0 - beta_one) * gradient
    new_two = beta_two * moment_two + (1.0 - beta_two) * gradient * gradient
    update = new_one / (jnp.sqrt(new_two) + epsilon) + weight_decay * kv_weight
    weight_sums, update_sums = lax.psum(
        (jnp.sum(kv_weight * kv_weight, axis=(1, 2)), jnp.sum(update * update, axis=(1, 2))),
        ("context", "dp"),
    )
    trust_ratio = jnp.sqrt(weight_sums) / (jnp.sqrt(update_sums) + epsilon)
    new_weight = kv_weight - learn_rate * trust_ratio[:, None, None] * update
    query_grad = query_acc.reshape(query_rows, heads * head_dim).astype(jnp.bfloat16)
    return (query_grad[None], kv_low[None], new_weight, new_one, new_two, trust_ratio)


def solution(mesh):
    in_specs = (
        P("dp", "context", None),
        P("dp", "context", None),
        P("dp", "context", None),
        P("dp", "context", None),
        P("dp", "context", None),
        P("dp", "context", None),
        P("dp", "context"),
        P(),
        P(None, ("context", "dp"), None),
        P(None, ("context", "dp"), None),
        P(None, ("context", "dp"), None),
    )
    out_specs = (
        P("dp", "context", None),
        P("dp", "context", None),
        P(None, ("context", "dp"), None),
        P(None, ("context", "dp"), None),
        P(None, ("context", "dp"), None),
        P(),
    )
    return jax.shard_map(
        on_device, mesh=mesh, in_specs=in_specs, out_specs=out_specs, check_vma=False
    )
```

profile of v0, /device:TPU:1, one launch (start us, length us, event | category | flops | bytes accessed | tf_op | source)
XLA Modules:
  0.0 2465.9 jit_solution(11954934748327105841)
XLA Ops:
  9.6 132.9 %all_gather.10 = s32[1,8192]{1,0:T(1,128)S(1)} all-gather(s32[1,128]{1,0:T(1,128)} %param.21), channel_id=1, replica_groups=mesh['context'=64,'dp'=4] {'context'}, dimensions={1}, use_global_device_ids=true | all-gather | bytes 33280 | tf_op jit(solution)/shard_map/all_gather | solution.py:53
  146.8 122.7 %all-gather.3.cloned.1.call-done = bf16[1,8192,128]{2,1,0:T(8,128)(2,1)} async-done(((bf16[1,128,128]{2,1,0:T(8,128)(2,1)}), bf16[1,8192,128]{2,1,0:T(8,128)(2,1)}) %all-gather.3.cloned.1.call-update) | async-done | bytes 2097168 | tf_op jit(solution)/shard_map/all_gather | solution.py:95
  269.5 38.9 %while.36 = (s32[]{:T(128)}, f32[128,8]{0,1:T(8,128)S(1)}, f32[128,8]{0,1:T(8,128)S(1)}, s32[128]{0:T(128)S(1)}, s32[128]{0:T(128)S(1)}, /*index=5*/s32[8192]{0:...) while((s32[]{:T(128)}, f32[128,8]{0,1:T(8,128)S(1)}, ...), condition=%wide.region_5.6_spmd.clone, body=%wide.region_1.0_spmd.clone.sunk | while | flops 138300928 | bytes 4857550 | solution.py:93
  308.4 260.5 %all-gather.5.cloned.1.call-done = bf16[1,8192,128]{2,1,0:T(8,128)(2,1)} async-done(((bf16[1,128,128]{2,1,0:T(8,128)(2,1)}), bf16[1,8192,128]{2,1,0:T(8,128)(2,1)}) %all-gather.5.cloned.1.call-update) | async-done | bytes 2097168 | tf_op jit(solution)/shard_map/all_gather | solution.py:96
  569.0 3.8 broadcast_in_dim.215.clone
  572.7 149.1 %while.37 = (s32[]{:T(128)}, f32[128,8,128]{2,0,1:T(8,128)}, f32[8192,256]{1,0:T(8,128)}, s32[128]{0:T(128)S(1)}, s32[128]{0:T(128)S(1)}, /*index=5*/s32[8192]{0...) while((s32[]{:T(128)}, f32[128,8,128]{2,0,1:T(8,128)}, ...), condition=%wide.region_9.10_spmd.clone, body=%wide.region_7.9_spmd.clone.sunk | while | flops 676215296 | bytes 23621456 | solution.py:127
  574.6 1.6 bitcast_select_fusion.3
  583.9 1.6 bitcast_select_fusion.3
  593.2 1.6 bitcast_select_fusion.3
  602.5 1.6 bitcast_select_fusion.3
  611.8 1.6 bitcast_select_fusion.3
  621.2 1.6 bitcast_select_fusion.3
  630.5 1.6 bitcast_select_fusion.3
  639.8 1.6 bitcast_select_fusion.3
  649.1 1.6 bitcast_select_fusion.3
  667.8 1.6 bitcast_select_fusion.3
  677.1 1.6 bitcast_select_fusion.3
  686.4 1.6 bitcast_select_fusion.3
  695.7 1.6 bitcast_select_fusion.3
  721.9 327.7 %reduce-scatter.5.cloned.1.call-done = f32[128,256]{1,0:T(8,128)} async-done(((f32[8192,256]{1,0:T(8,128)}), f32[128,256]{1,0:T(8,128)}) %reduce-scatter.5.cloned.1.call-update) | async-done | bytes 131088 | tf_op jit(solution)/shard_map/reduce_scatter | solution.py:128
  1049.7 5.4 convolution_bitcast_fusion.2
  1055.1 9.0 copy.66
  1066.8 1311.9 %reduce-scatter.7.cloned.1.call-done = f32[32,256]{1,0:T(8,128)} async-done(((f32[8192,256]{1,0:T(8,128)}), f32[32,256]{1,0:T(8,128)}) %reduce-scatter.7.cloned.1.call-update) | async-done | bytes 32784
  2380.0 78.2 %all-reduce = (f32[2]{0:T(128)S(1)}, f32[2]{0:T(128)S(1)}) all-reduce(f32[2]{0:T(128)S(1)} %get-tuple-element.652, f32[2]{0:T(128)S(1)} %get-tuple-element.651), channel_id=1, replica_groups=mesh['context'=64,'dp'=4] {'context','dp'}, use_global_device_ids=true, to_apply=%region_15.16 | all-reduce | flops 4 | bytes 32 | tf_op jit(solution)/shard_map/psum | solution.py:143
  (537 shorter events, 176.5 us)
Async XLA Ops:
  7.2 1042.5 %copy-start = (bf16[1,128,8192]{2,1,0:T(8,128)(2,1)S(1)}, bf16[1,128,8192]{2,1,0:T(8,128)(2,1)}, u32[]{:S(2)}) copy-start(bf16[1,128,8192]{2,1,0:T(8,128)(2,1)} %param.20) | copy-start | bytes 6291460
  7.2 262.3 %copy-start.11 = (s32[128]{0:T(128)S(1)}, s32[128]{0:T(128)}, u32[]{:S(2)}) copy-start(s32[128]{0:T(128)} %param.22) | copy-start | bytes 1540
  7.2 262.3 %copy-start.10 = (s32[1,128]{1,0:T(1,128)S(1)}, s32[1,128]{1,0:T(1,128)}, u32[]{:S(2)}) copy-start(s32[1,128]{1,0:T(1,128)} %param.21) | copy-start | bytes 1540
  7.2 262.3 %all-gather.3.cloned.1.call-start = ((), (), s32[]{:S(2)}) async-start(), calls=%async_computation.2 | async-start | bytes 2129920 | tf_op jit(solution)/shard_map/all_gather | solution.py:95
  7.9 561.0 %all-gather.5.cloned.1.call-start = ((), (), s32[]{:S(2)}) async-start(), calls=%async_computation.3 | async-start | bytes 2129920 | tf_op jit(solution)/shard_map/all_gather | solution.py:96
  8.7 1041.0 %reduce-scatter.5.cloned.1.call-start = ((), (), s32[]{:S(2)}) async-start(), calls=%async_computation.4 | async-start | bytes 8519680 | tf_op jit(solution)/shard_map/reduce_scatter | solution.py:128
  576.6 1.9 copy-start.1
  585.9 1.9 copy-start.1
  604.6 1.9 copy-start.1
  613.9 1.9 copy-start.1
  623.2 1.9 copy-start.1
  632.6 1.9 copy-start.1
  641.9 1.9 copy-start.1
  651.2 1.9 copy-start.1
  660.5 1.9 copy-start.1
  679.1 1.9 copy-start.1
  707.1 1.9 copy-start.1
  721.9 1656.8 %reduce-scatter.7.cloned.1.call-start = ((), (), s32[]{:S(2)}) async-start(), calls=%async_computation.5 | async-start | bytes 8421376
  1064.1 2.1 copy-start.6
  1064.1 1315.7 %copy-start.7 = (f32[2,32,128]{2,1,0:T(8,128)S(1)}, f32[2,32,128]{2,1,0:T(8,128)}, u32[]{:S(2)}) copy-start(f32[2,32,128]{2,1,0:T(8,128)} %param.23) | copy-start | bytes 98308
  1064.1 1315.7 %copy-start.12 = (f32[2,32,128]{2,1,0:T(8,128)S(1)}, f32[2,32,128]{2,1,0:T(8,128)}, u32[]{:S(2)}) copy-start(f32[2,32,128]{2,1,0:T(8,128)} %param.25) | copy-start | bytes 98308
  1064.1 1315.7 %copy-start.13 = (f32[2,32,128]{2,1,0:T(8,128)S(1)}, f32[2,32,128]{2,1,0:T(8,128)}, u32[]{:S(2)}) copy-start(f32[2,32,128]{2,1,0:T(8,128)} %param.24) | copy-start | bytes 98308
  2380.0 79.4 %copy-start.8 = (f32[2,32,128]{2,1,0:T(8,128)}, f32[2,32,128]{2,1,0:T(8,128)S(1)}, u32[]{:S(2)}) copy-start(f32[2,32,128]{2,1,0:T(8,128)S(1)} %get-tuple-element.701) | copy-start | bytes 98308
  2380.0 79.4 %copy-start.9 = (f32[2,32,128]{2,1,0:T(8,128)}, f32[2,32,128]{2,1,0:T(8,128)S(1)}, u32[]{:S(2)}) copy-start(f32[2,32,128]{2,1,0:T(8,128)S(1)} %get-tuple-element.702) | copy-start | bytes 98308
  (39 other events, 47.0 us)
Sparse Core Ops, SparseCore 0:
  9.8 259.6 all-gather.2
  271.3 297.6 all-gather.4
  722.0 327.6 reduce-scatter.4
  1064.2 1314.4 reduce-scatter.6
where the time goes:
time: 2470 us
  waiting for transfers between devices  2020 us (82%)
  blocking collectives  211 us (9%)
  matrix products  115 us (5%)
  local copies, waits for them, and re-layouts  72.3 us (3%)
  other arithmetic  26.4 us (1%)
    unnamed x5, waiting for transfers between devices  1310 us
    reduce_scatter x1, waiting for transfers between devices, on_device(): lax.psum_scatter(kv_acc, 'context', scatter_dimension=0, tiled=True)  328 us
    all_gather x1, waiting for transfers between devices, on_device(): value_piece = lax.all_gather(value_states, 'context', axis=1, tiled=True)  261 us
    all_gather x1, blocking collectives, on_device(): all_segments = lax.all_gather(segment_ids, 'context', axis=1, tiled=True)[0]  133 us
    all_gather x1, waiting for transfers between devices, on_device(): fold_key_piece = lax.all_gather(key_states, 'context', axis=1, tiled=True)  123 us
    psum x1, blocking collectives, on_device(): lax.psum((jnp.sum(kv_weight * kv_weight, axis=(1, 2)), jnp.sum(update * u...  78.2 us
  transfers between devices with their start and end apart: 4, of which 4 were waited for; matrix products, arithmetic and copies ran while one was open for 2% of the time, Pallas kernels for 0%

commit v1 on v0

v1 whole, which is shorter than its diff:
```python
import functools

import jax
import jax.numpy as jnp
from jax import lax
from jax.experimental import pallas as pl
from jax.experimental.pallas import tpu as pltpu
from jax.sharding import PartitionSpec as P

beta_one = 0.9
beta_two = 0.999
epsilon = 1e-06
weight_decay = 0.01
learn_rate = 0.01

HEADS = 8
DIM = 128
SPAN = 64
ROWS = 128
LANES = HEADS * SPAN
BLOCK = 256
KEYS = 2048
SCALE = DIM ** (-0.5)
LOG2E = 1.4426950408889634
MESH = pl.DeviceIdType.MESH
VMEM = pltpu.VMEM
F32 = jnp.float32
BF16 = jnp.bfloat16


def vmem_spec():
    return pl.BlockSpec(memory_space=pltpu.VMEM)


def any_spec():
    return pl.BlockSpec(memory_space=pl.ANY)


def smem_spec():
    return pl.BlockSpec(memory_space=pltpu.SMEM)


def greet(peers):
    barrier = pltpu.get_barrier_semaphore()
    for peer in peers:
        pl.semaphore_signal(barrier, inc=1, device_id=peer, device_id_type=MESH)
    return barrier


def send(src, dst, send_sem, recv_sem, peer):
    copy = pltpu.make_async_remote_copy(
        src_ref=src, dst_ref=dst, send_sem=send_sem, recv_sem=recv_sem,
        device_id=peer, device_id_type=MESH,
    )
    copy.start()
    return copy


def arrived(dst, sem):
    pltpu.make_async_copy(dst, dst, sem).wait()


def place():
    me = lax.axis_index("context")
    dp = lax.axis_index("dp")
    return me, dp, me // 16, me % 16


def x_peers(me, dp, x, rest):
    return [(lax.rem(x + i, 4) * 16 + rest, dp) for i in range(1, 4)]


def rest_peers(me, dp, x, rest):
    return [(x * 16 + lax.rem(rest + i, 16), dp) for i in range(1, 16)]


def gather_kernel(
    q_ref, g_ref, o_ref, k_ref, v_ref, seg_ref, segk_ref,
    qg_ref, gg_ref, kvg_ref, auxg_ref, segg_ref,
    qbuf, gbuf, kvbuf, auxbuf,
    x_send, x_recv, r_send, r_recv, own_sem,
):
    me, dp, x, rest = place()
    xs = x_peers(me, dp, x, rest)
    rs = rest_peers(me, dp, x, rest)
    barrier = greet(xs + rs)
    kvbuf[0] = k_ref[...]
    kvbuf[1] = v_ref[...]
    for span in range(2):
        rows = pl.ds(span * SPAN, SPAN)
        pieces = []
        for h in range(HEADS):
            cols = pl.ds(h * DIM, DIM)
            qbuf[span, pl.ds(h * SPAN, SPAN), :] = q_ref[rows, cols]
            grad = g_ref[rows, cols]
            gbuf[span, pl.ds(h * SPAN, SPAN), :] = grad
            pieces.append(grad.astype(F32) * o_ref[rows, cols].astype(F32))
        product = jnp.concatenate(pieces, axis=0)
        auxbuf[pl.ds(span, 1), :] = jnp.sum(product.T, axis=0, keepdims=True)
    auxbuf[pl.ds(2, 2), :] = seg_ref[...]
    auxbuf[pl.ds(4, 4), :] = jnp.zeros((4, LANES), F32)
    pl.semaphore_wait(barrier, len(xs) + len(rs))
    copies = []
    two = pl.ds(2 * x, 2)
    for i, peer in enumerate(rs):
        copies.append(send(kvbuf, kvg_ref.at[rest], r_send.at[0, i], r_recv.at[0, rest], peer))
        copies.append(send(segk_ref, segg_ref.at[rest], r_send.at[1, i], r_recv.at[1, rest], peer))
        if i < 3:
            copies.append(send(qbuf, qg_ref.at[two], x_send.at[0, i], x_recv.at[0, x], xs[i]))
            copies.append(send(gbuf, gg_ref.at[two], x_send.at[1, i], x_recv.at[1, x], xs[i]))
            copies.append(send(auxbuf, auxg_ref.at[x], x_send.at[2, i], x_recv.at[2, x], xs[i]))
    own = [
        pltpu.make_async_copy(kvbuf, kvg_ref.at[rest], own_sem.at[0]),
        pltpu.make_async_copy(segk_ref, segg_ref.at[rest], own_sem.at[1]),
        pltpu.make_async_copy(qbuf, qg_ref.at[two], own_sem.at[2]),
        pltpu.make_async_copy(gbuf, gg_ref.at[two], own_sem.at[3]),
        pltpu.make_async_copy(auxbuf, auxg_ref.at[x], own_sem.at[4]),
    ]
    for copy in own:
        copy.start()
    for copy in own:
        copy.wait()
    for i in range(1, 16):
        slot = lax.rem(rest + i, 16)
        arrived(kvg_ref.at[slot], r_recv.at[0, slot])
        arrived(segg_ref.at[slot], r_recv.at[1, slot])
    for i in range(1, 4):
        slot = lax.rem(x + i, 4)
        pair = pl.ds(2 * slot, 2)
        arrived(qg_ref.at[pair], x_recv.at[0, slot])
        arrived(gg_ref.at[pair], x_recv.at[1, slot])
        arrived(auxg_ref.at[slot], x_recv.at[2, slot])
    for copy in copies:
        copy.wait_send()


def gather(queries, out_grad, attn_out, key_states, value_states, seg_rows, seg_keys):
    return pl.pallas_call(
        gather_kernel,
        out_shape=(
            jax.ShapeDtypeStruct((8, LANES, DIM), BF16),
            jax.ShapeDtypeStruct((8, LANES, DIM), BF16),
            jax.ShapeDtypeStruct((16, 2, ROWS, DIM), BF16),
            jax.ShapeDtypeStruct((4, 8, LANES), F32),
            jax.ShapeDtypeStruct((16, 8, ROWS), F32),
        ),
        in_specs=[vmem_spec()] * 7,
        out_specs=(any_spec(),) * 5,
        scratch_shapes=[
            VMEM((2, LANES, DIM), BF16),
            VMEM((2, LANES, DIM), BF16),
            VMEM((2, ROWS, DIM), BF16),
            VMEM((8, LANES), F32),
            pltpu.SemaphoreType.DMA((3, 3)),
            pltpu.SemaphoreType.DMA((3, 4)),
            pltpu.SemaphoreType.DMA((2, 15)),
            pltpu.SemaphoreType.DMA((2, 16)),
            pltpu.SemaphoreType.DMA((5,)),
        ],
        compiler_params=pltpu.CompilerParams(
            collective_id=0, has_side_effects=True, vmem_limit_bytes=32 * 1024 * 1024
        ),
        name="gather_rows",
    )(queries, out_grad, attn_out, key_states, value_states, seg_rows, seg_keys)


def key_counts(segg_ref):
    seg = segg_ref[:, 0, :]
    return [jnp.sum((seg < d - 0.5).astype(F32)).astype(jnp.int32) for d in (1, 2, 3)]


def span_range(meta_ref, auxg_ref, counts, s):
    slot = s // 2
    seg = auxg_ref[slot, pl.ds(2 + s % 2, 1), :]
    low = jnp.where(
        seg > 2.5, counts[2], jnp.where(seg > 1.5, counts[1], jnp.where(seg > 0.5, counts[0], 0))
    )
    x = lax.axis_index("context") // 16
    own = (slot == x).astype(jnp.int32)
    base = meta_ref[32 + s] * SPAN
    row = lax.broadcasted_iota(jnp.int32, (1, LANES), 1) % SPAN
    high = base + own * (row + 1)
    low_min, low_max = jnp.min(low), jnp.max(low)
    high_min, high_max = base + own, base + own * SPAN
    first = low_min // BLOCK
    last = (high_max + BLOCK - 1) // BLOCK
    return low, high, low_max, high_min, first, last


def inside(low, high, block):
    place_of = block * BLOCK + lax.broadcasted_iota(jnp.int32, (BLOCK, LANES), 0)
    return (place_of >= low) & (place_of < high)


def sort_keys(meta_ref, kvg_ref, which, sorted_ref):
    def step(t, carry):
        rank = meta_ref[t]
        source = pl.multiple_of((t % 2) * SPAN, SPAN)
        target = pl.multiple_of(rank * SPAN, SPAN)
        sorted_ref[pl.ds(target, SPAN), :] = kvg_ref[t // 2, which, pl.ds(source, SPAN), :]
        return carry

    lax.fori_loop(0, 32, step, 0)


def stats_kernel(meta_ref, qg_ref, kvg_ref, auxg_ref, segg_ref, out_ref, ks, qt, top, total):
    sort_keys(meta_ref, kvg_ref, 0, ks)
    counts = key_counts(segg_ref)

    def span_step(s, carry):
        low, high, low_max, high_min, first, last = span_range(meta_ref, auxg_ref, counts, s)
        qt[...] = qg_ref[s].T
        top[...] = jnp.full((1, LANES), -1e30, F32)
        total[...] = jnp.zeros((1, LANES), F32)

        def tile(block, masked):
            offset = pl.multiple_of(block * BLOCK, BLOCK)
            scores = jnp.dot(
                ks[pl.ds(offset, BLOCK), :], qt[...], preferred_element_type=F32
            ) * (SCALE * LOG2E)
            if masked:
                seen = inside(low, high, block)
                scores = jnp.where(seen, scores, -1e30)
            old = top[...]
            new = jnp.maximum(old, jnp.max(scores, axis=0, keepdims=True))
            weights = jnp.exp2(scores - new)
            if masked:
                weights = jnp.where(seen, weights, 0.0)
            total[...] = total[...] * jnp.exp2(old - new) + jnp.sum(weights, axis=0, keepdims=True)
            top[...] = new

        def block_step(block, carry):
            edge = (block * BLOCK < low_max) | ((block + 1) * BLOCK > high_min)

            @pl.when(edge)
            def _():
                tile(block, True)

            @pl.when(jnp.logical_not(edge))
            def _():
                tile(block, False)

            return carry

        lax.fori_loop(first, last, block_step, 0)
        out_ref[0, pl.ds(s, 1), :] = top[...]
        out_ref[1, pl.ds(s, 1), :] = total[...]
        return carry

    lax.fori_loop(0, 8, span_step, 0)


def stats(meta, qg, kvg, auxg, segg):
    return pl.pallas_call(
        stats_kernel,
        out_shape=jax.ShapeDtypeStruct((2, 8, LANES), F32),
        in_specs=[smem_spec()] + [vmem_spec()] * 4,
        out_specs=vmem_spec(),
        scratch_shapes=[
            VMEM((KEYS, DIM), BF16),
            VMEM((DIM, LANES), BF16),
            VMEM((1, LANES), F32),
            VMEM((1, LANES), F32),
        ],
        compiler_params=pltpu.CompilerParams(vmem_limit_bytes=48 * 1024 * 1024),
        name="softmax_totals",
    )(meta, qg, kvg, auxg, segg)


def combine_kernel(part_ref, out_ref, got, send_sem, recv_sem):
    me, dp, x, rest = place()
    xs = x_peers(me, dp, x, rest)
    barrier = greet(xs)
    got[x] = part_ref[...]
    pl.semaphore_wait(barrier, len(xs))
    copies = [
        send(part_ref, got.at[x], send_sem.at[i], recv_sem.at[x], peer)
        for i, peer in enumerate(xs)
    ]
    for i in range(1, 4):
        slot = lax.rem(x + i, 4)
        arrived(got.at[slot], recv_sem.at[slot])
    for copy in copies:
        copy.wait_send()
    top = jnp.maximum(
        jnp.maximum(got[0, 0], got[1, 0]), jnp.maximum(got[2, 0], got[3, 0])
    )
    total = jnp.zeros_like(top)
    for slot in range(4):
        total = total + got[slot, 1] * jnp.exp2(got[slot, 0] - top)
    out_ref[...] = top + jnp.log(total) * LOG2E


def combine(part):
    return pl.pallas_call(
        combine_kernel,
        out_shape=jax.ShapeDtypeStruct((8, LANES), F32),
        in_specs=[vmem_spec()],
        out_specs=vmem_spec(),
        scratch_shapes=[
            VMEM((4, 2, 8, LANES), F32),
            pltpu.SemaphoreType.DMA((3,)),
            pltpu.SemaphoreType.DMA((4,)),
        ],
        compiler_params=pltpu.CompilerParams(collective_id=1, has_side_effects=True),
        name="combine_totals",
    )(part)


def grads_kernel(
    meta_ref, qg_ref, gg_ref, kvg_ref, auxg_ref, segg_ref, log_ref,
    dq_ref, dkv_ref,
    ks, vs, kt, qt, gt, dqt, dk, dv,
):
    sort_keys(meta_ref, kvg_ref, 0, ks)
    sort_keys(meta_ref, kvg_ref, 1, vs)
    for b in range(KEYS // BLOCK):
        kt[b] = ks[pl.ds(b * BLOCK, BLOCK), :].T
    dk[...] = jnp.zeros_like(dk)
    dv[...] = jnp.zeros_like(dv)
    counts = key_counts(segg_ref)

    def span_step(s, carry):
        low, high, low_max, high_min, first, last = span_range(meta_ref, auxg_ref, counts, s)
        qt[...] = qg_ref[s].T
        gt[...] = gg_ref[s].T
        dqt[...] = jnp.zeros_like(dqt)
        log_total = log_ref[pl.ds(s, 1), :]
        delta = auxg_ref[s // 2, pl.ds(s % 2, 1), :]

        def tile(block, masked):
            rows = pl.ds(pl.multiple_of(block * BLOCK, BLOCK), BLOCK)
            scores = jnp.dot(ks[rows, :], qt[...], preferred_element_type=F32)
            probs = jnp.exp2(scores * (SCALE * LOG2E) - log_total)
            if masked:
                probs = jnp.where(inside(low, high, block), probs, 0.0)
            prob_grad = jnp.dot(vs[rows, :], gt[...], preferred_element_type=F32)
            score_grad = (SCALE * probs * (prob_grad - delta)).astype(BF16)
            dv[rows, :] += jnp.dot(probs.astype(BF16), gg_ref[s], preferred_element_type=F32)
            dk[rows, :] += jnp.dot(score_grad, qg_ref[s], preferred_element_type=F32)
            dqt[...] += jnp.dot(kt[block], score_grad, preferred_element_type=F32)

        def block_step(block, carry):
            edge = (block * BLOCK < low_max) | ((block + 1) * BLOCK > high_min)

            @pl.when(edge)
            def _():
                tile(block, True)

            @pl.when(jnp.logical_not(edge))
            def _():
                tile(block, False)

            return carry

        lax.fori_loop(first, last, block_step, 0)
        dq_ref[s] = dqt[...].T.astype(BF16)
        return carry

    lax.fori_loop(0, 8, span_step, 0)

    def unsort(t, carry):
        source = pl.ds(pl.multiple_of(meta_ref[t] * SPAN, SPAN), SPAN)
        target = pl.ds(pl.multiple_of((t % 2) * SPAN, SPAN), SPAN)
        dkv_ref[t // 2, target, pl.ds(0, DIM)] = dk[source, :].astype(BF16)
        dkv_ref[t // 2, target, pl.ds(DIM, DIM)] = dv[source, :].astype(BF16)
        return carry

    lax.fori_loop(0, 32, unsort, 0)


def grads(meta, qg, gg, kvg, auxg, segg, log_total):
    return pl.pallas_call(
        grads_kernel,
        out_shape=(
            jax.ShapeDtypeStruct((8, LANES, DIM), BF16),
            jax.ShapeDtypeStruct((16, ROWS, 2 * DIM), BF16),
        ),
        in_specs=[smem_spec()] + [vmem_spec()] * 6,
        out_specs=(vmem_spec(),) * 2,
        scratch_shapes=[
            VMEM((KEYS, DIM), BF16),
            VMEM((KEYS, DIM), BF16),
            VMEM((KEYS // BLOCK, DIM, BLOCK), BF16),
            VMEM((DIM, LANES), BF16),
            VMEM((DIM, LANES), BF16),
            VMEM((DIM, LANES), F32),
            VMEM((KEYS, DIM), F32),
            VMEM((KEYS, DIM), F32),
        ],
        compiler_params=pltpu.CompilerParams(vmem_limit_bytes=56 * 1024 * 1024),
        name="attention_grads",
    )(meta, qg, gg, kvg, auxg, segg, log_total)


def tail_kernel(
    dkv_ref, dq_ref, act_ref, w_ref, m1_ref, m2_ref,
    qgrad_ref, kvgrad_ref, nw_ref, n1_ref, n2_ref, trust_ref,
    dkv_in, dq_in, act_in, kv_in, partial, g_in, a_in, a_msg, b_in, b_msg,
    r_send, r_recv, x_send, x_recv, act_send, act_recv, kv_send, kv_recv,
    g_send, g_recv, a_send, a_recv, b_send, b_recv, own_sem,
):
    me, dp, x, rest = place()
    y_lo, z = rest // 8, rest % 8
    y_hi, core = dp // 2, dp % 2
    column = x * 4 + y_lo * 2 + y_hi
    line = z * 2 + core
    xs = x_peers(me, dp, x, rest)
    rs = rest_peers(me, dp, x, rest)

    def in_column(index):
        return ((index // 4) * 16 + (index // 2 % 2) * 8 + z, (index % 2) * 2 + core)

    def in_line(index):
        return (x * 16 + y_lo * 8 + index // 2, y_hi * 2 + index % 2)

    columns = [in_column(lax.rem(column + i, 16)) for i in range(1, 16)]
    lines = [in_line(lax.rem(line + i, 16)) for i in range(1, 16)]
    greeted = [
        (x * 16 + y_lo * 8 + lax.rem(z + i // 4, 8), lax.rem(dp + i % 4, 4)) for i in range(1, 32)
    ]
    greeted += [(x * 16 + (1 - y_lo) * 8 + i, dp) for i in range(8)]
    greeted += [
        (lax.rem(x + i, 4) * 16 + j * 8 + z, k * 2 + core)
        for i in range(1, 4) for j in range(2) for k in range(2)
    ]
    greeted += [(x * 16 + (1 - y_lo) * 8 + z, (1 - y_hi) * 2 + core)]
    barrier = greet(greeted)
    own = [
        pltpu.make_async_copy(dkv_ref.at[rest], dkv_in.at[rest], own_sem.at[0]),
        pltpu.make_async_copy(dq_ref.at[pl.ds(2 * x, 2)], dq_in.at[x], own_sem.at[1]),
        pltpu.make_async_copy(
            act_ref.at[:, pl.ds(pl.multiple_of(column * LANES, LANES), LANES)],
            act_in.at[0], own_sem.at[2],
        ),
    ]
    for copy in own:
        copy.start()
    pl.semaphore_wait(barrier, len(greeted))

    copies = []
    for i, peer in enumerate(rs):
        there = lax.rem(rest + i + 1, 16)
        copies.append(
            send(dkv_ref.at[there], dkv_in.at[rest], r_send.at[i], r_recv.at[rest], peer)
        )
    for i, peer in enumerate(xs):
        there = lax.rem(x + i + 1, 4)
        copies.append(
            send(dq_ref.at[pl.ds(2 * there, 2)], dq_in.at[x], x_send.at[i], x_recv.at[x], peer)
        )
    for i, peer in enumerate(columns):
        there = lax.rem(column + i + 1, 16)
        piece = act_ref.at[:, pl.ds(pl.multiple_of(there * LANES, LANES), LANES)]
        copies.append(
            send(piece, act_in.at[i + 1], act_send.at[i], act_recv.at[i], peer)
        )

    for copy in own:
        copy.wait()
    for i in range(1, 16):
        slot = lax.rem(rest + i, 16)
        arrived(dkv_in.at[slot], r_recv.at[slot])
    kv_sum = dkv_in[0].astype(F32)
    for slot in range(1, 16):
        kv_sum = kv_sum + dkv_in[slot].astype(F32)
    kv_low = kv_sum.astype(BF16)
    kv_in[0] = kv_low
    kvgrad_ref[...] = kv_low
    for i, peer in enumerate(columns):
        copies.append(send(kv_in.at[0], kv_in.at[i + 1], kv_send.at[i], kv_recv.at[i], peer))

    for i in range(1, 4):
        slot = lax.rem(x + i, 4)
        arrived(dq_in.at[slot], x_recv.at[slot])
    for span in range(2):
        for h in range(HEADS):
            rows = pl.ds(h * SPAN, SPAN)
            summed = dq_in[0, span, rows, :].astype(F32)
            for slot in range(1, 4):
                summed = summed + dq_in[slot, span, rows, :].astype(F32)
            qgrad_ref[pl.ds(span * SPAN, SPAN), pl.ds(h * DIM, DIM)] = summed.astype(BF16)

    total = jnp.zeros((2 * DIM, LANES), F32)
    for i in range(16):
        if i > 0:
            arrived(act_in.at[i], act_recv.at[i - 1])
            arrived(kv_in.at[i], kv_recv.at[i - 1])
        total = total + jnp.dot(kv_in[i].T, act_in[i], preferred_element_type=F32)
    partial[...] = total.T

    here = z // 4 == y_hi

    def owner(i):
        there_z = lax.rem(z % 4 + i // 4, 4)
        there_dp = lax.rem(dp + i % 4, 4)
        rows = pl.ds(pl.multiple_of((there_z * 4 + there_dp) * 32, 32), 32)
        return partial.at[rows], (x * 16 + y_lo * 8 + y_hi * 4 + there_z, there_dp)

    def to_owner(i):
        source, peer = owner(i)
        return pltpu.make_async_remote_copy(
            src_ref=source, dst_ref=g_in.at[line], send_sem=g_send.at[i],
            recv_sem=g_recv.at[line], device_id=peer, device_id_type=MESH,
        )

    for i in range(1, 16):
        to_owner(i).start()

    @pl.when(here)
    def _():
        pltpu.make_async_copy(owner(0)[0], g_in.at[line], g_recv.at[line]).start()

    @pl.when(jnp.logical_not(here))
    def _():
        to_owner(0).start()

    for slot in range(16):
        arrived(g_in.at[slot], g_recv.at[slot])
    gradient = g_in[0]
    for slot in range(1, 16):
        gradient = gradient + g_in[slot]

    sums, updates = [], []
    for p in range(2):
        grad = gradient[:, p * DIM:(p + 1) * DIM]
        weight = w_ref[p]
        one = beta_one * m1_ref[p] + (1.0 - beta_one) * grad
        two = beta_two * m2_ref[p] + (1.0 - beta_two) * grad * grad
        n1_ref[p] = one
        n2_ref[p] = two
        update = one / (jnp.sqrt(two) + epsilon) + weight_decay * weight
        updates.append(update)
        sums.append(jnp.sum(weight * weight, axis=0, keepdims=True))
        sums.append(jnp.sum(update * update, axis=0, keepdims=True))
    a_msg[...] = jnp.concatenate(sums + [jnp.zeros((4, DIM), F32)], axis=0)
    a_in[column] = a_msg[...]
    for i, peer in enumerate(columns):
        copies.append(send(a_msg, a_in.at[column], a_send.at[i], a_recv.at[column], peer))
    for i in range(1, 16):
        slot = lax.rem(column + i, 16)
        arrived(a_in.at[slot], a_recv.at[slot])
    summed = a_in[0]
    for slot in range(1, 16):
        summed = summed + a_in[slot]
    b_msg[...] = summed
    b_in[line] = summed
    for i, peer in enumerate(lines):
        copies.append(send(b_msg, b_in.at[line], b_send.at[i], b_recv.at[line], peer))
    for i in range(1, 16):
        slot = lax.rem(line + i, 16)
        arrived(b_in.at[slot], b_recv.at[slot])
    summed = b_in[0]
    for slot in range(1, 16):
        summed = summed + b_in[slot]
    norms = jnp.sqrt(jnp.sum(summed, axis=1, keepdims=True))
    ratios = []
    for p in range(2):
        ratio = norms[2 * p:2 * p + 1] / (norms[2 * p + 1:2 * p + 2] + epsilon)
        ratios.append(ratio)
        nw_ref[p] = w_ref[p] - learn_rate * ratio * updates[p]
    trust_ref[...] = jnp.concatenate(
        [jnp.broadcast_to(ratio, (1, DIM)) for ratio in ratios] + [jnp.zeros((6, DIM), F32)], axis=0
    )
    for copy in copies:
        copy.wait_send()
    for i in range(1, 16):
        to_owner(i).wait_send()

    @pl.when(jnp.logical_not(here))
    def _():
        to_owner(0).wait_send()


def tail(dkv, dq, act, kv_weight, moment_one, moment_two):
    state = jax.ShapeDtypeStruct((2, 32, DIM), F32)
    dma = pltpu.SemaphoreType.DMA
    return pl.pallas_call(
        tail_kernel,
        out_shape=(
            jax.ShapeDtypeStruct((ROWS, HEADS * DIM), BF16),
            jax.ShapeDtypeStruct((ROWS, 2 * DIM), BF16),
            state, state, state,
            jax.ShapeDtypeStruct((8, DIM), F32),
        ),
        in_specs=[any_spec()] * 3 + [vmem_spec()] * 3,
        out_specs=(vmem_spec(),) * 6,
        scratch_shapes=[
            VMEM((16, ROWS, 2 * DIM), BF16),
            VMEM((4, 2, LANES, DIM), BF16),
            VMEM((16, ROWS, LANES), BF16),
            VMEM((16, ROWS, 2 * DIM), BF16),
            VMEM((LANES, 2 * DIM), F32),
            VMEM((16, 32, 2 * DIM), F32),
            VMEM((16, 8, DIM), F32),
            VMEM((8, DIM), F32),
            VMEM((16, 8, DIM), F32),
            VMEM((8, DIM), F32),
            dma((15,)), dma((16,)),
            dma((3,)), dma((4,)),
            dma((15,)), dma((15,)),
            dma((15,)), dma((15,)),
            dma((16,)), dma((16,)),
            dma((15,)), dma((16,)),
            dma((15,)), dma((16,)),
            dma((3,)),
        ],
        compiler_params=pltpu.CompilerParams(
            collective_id=2, has_side_effects=True, vmem_limit_bytes=48 * 1024 * 1024
        ),
        name="reduce_and_update",
    )(dkv, dq, act, kv_weight, moment_one, moment_two)


def on_device(
    queries,
    key_states,
    value_states,
    attn_out,
    out_grad,
    activations,
    segment_ids,
    span_order,
    kv_weight,
    moment_one,
    moment_two,
):
    me = lax.axis_index("context")
    x, rest = me // 16, me % 16
    local = lax.dynamic_slice_in_dim(span_order, x * 32, 32, 0)
    mine = lax.dynamic_slice_in_dim(span_order.reshape(4, 16, 2), rest, 1, 1).reshape(8)
    asked = jnp.concatenate([local, mine])
    meta = jnp.sum((local[None, :] < asked[:, None]).astype(jnp.int32), axis=1)
    seg = segment_ids.astype(F32)
    seg_rows = jnp.tile(seg.reshape(2, 1, SPAN), (1, HEADS, 1)).reshape(2, LANES)
    seg_keys = jnp.broadcast_to(seg, (8, ROWS))
    qg, gg, kvg, auxg, segg = gather(
        queries[0], out_grad[0], attn_out[0], key_states[0], value_states[0], seg_rows, seg_keys
    )
    part = stats(meta, qg, kvg, auxg, segg)
    log_total = combine(part)
    dq, dkv = grads(meta, qg, gg, kvg, auxg, segg, log_total)
    query_grad, kv_grad, new_weight, new_one, new_two, trust = tail(
        dkv, dq, activations[0], kv_weight, moment_one, moment_two
    )
    return (query_grad[None], kv_grad[None], new_weight, new_one, new_two, trust[:2, 0])


def solution(mesh):
    in_specs = (
        P("dp", "context", None),
        P("dp", "context", None),
        P("dp", "context", None),
        P("dp", "context", None),
        P("dp", "context", None),
        P("dp", "context", None),
        P("dp", "context"),
        P(),
        P(None, ("context", "dp"), None),
        P(None, ("context", "dp"), None),
        P(None, ("context", "dp"), None),
    )
    out_specs = (
        P("dp", "context", None),
        P("dp", "context", None),
        P(None, ("context", "dp"), None),
        P(None, ("context", "dp"), None),
        P(None, ("context", "dp"), None),
        P(),
    )
    return jax.shard_map(
        on_device, mesh=mesh, in_specs=in_specs, out_specs=out_specs, check_vma=False
    )
```

time: 2470 us -> 199 us (0.08)
  waiting for transfers between devices: 2020 us -> 0 us
  blocking collectives: 211 us -> 0 us
  Pallas kernels: 0 us -> 182 us
  matrix products: 115 us -> 0 us
  local copies, waits for them, and re-layouts: 72.3 us -> 14.1 us
  other arithmetic: 26.4 us -> 1.5 us
    unnamed x5 -> x0, waiting for transfers between devices: 1310 us -> none
    all_gather x2 -> x0, waiting for transfers between devices: 383 us -> none  [the longest x1 261 us: on_device(): value_piece = lax.all_gather(value_states, 'context', axis=1, tiled=True)]
    reduce_scatter x1 -> x0, waiting for transfers between devices: 328 us -> none  [on_device(): lax.psum_scatter(kv_acc, 'context', scatter_dimension=0, tiled=True)]
    pallas_call x0 -> x5, Pallas kernels: none -> 182 us  [the longest x1 117 us: tail(): pl.pallas_call(tail_kernel, out_shape=(jax.ShapeDtypeStruct((ROWS, HEADS...]
    all_gather x1 -> x0, blocking collectives: 133 us -> none  [on_device(): all_segments = lax.all_gather(segment_ids, 'context', axis=1, tiled=True)[0]]
    dot_general x97 -> x0, matrix products: 115 us -> none  [the longest x32 47 us: score_block(): jnp.einsum('qhd,kd->qhk', query_heads, key_block, preferred_element_type=...]
    psum x1 -> x0, blocking collectives: 78.2 us -> none  [on_device(): lax.psum((jnp.sum(kv_weight * kv_weight, axis=(1, 2)), jnp.sum(update * u...]
  transfers between devices with their start and end apart: 4 -> 0, of which waited for: 4 -> 0; matrix products, arithmetic and copies ran while one was open for 2% -> 0% of each run, Pallas kernels for 0% -> 0%
where the time goes in v1:
time: 199 us
  Pallas kernels  182 us (91%)
  local copies, waits for them, and re-layouts  14.1 us (7%)
    pallas_call x1, Pallas kernels, tail(): pl.pallas_call(tail_kernel, out_shape=(jax.ShapeDtypeStruct((ROWS, HEADS...  117 us
    pallas_call x1, Pallas kernels, gather(): pl.pallas_call(gather_kernel, out_shape=(jax.ShapeDtypeStruct((8, LANES,...  35.6 us
    pallas_call x1, Pallas kernels, grads(): pl.pallas_call(grads_kernel, out_shape=(jax.ShapeDtypeStruct((8, LANES, D...  15.1 us
    unnamed x41, local copies, waits for them, and re-layouts  11.6 us
    pallas_call x1, Pallas kernels, stats(): pl.pallas_call(stats_kernel, out_shape=jax.ShapeDtypeStruct((2, 8, LANES)...  8.21 us
    pallas_call x1, Pallas kernels, combine(): pl.pallas_call(combine_kernel, out_shape=jax.ShapeDtypeStruct((8, LANES),...  6.08 us

profile of v1, /device:TPU:1, one launch (start us, length us, event | category | flops | bytes accessed | tf_op | source)
XLA Modules:
  0.0 198.6 jit_solution(11272569942413822060)
XLA Ops:
  0.7 0.7 dynamic_slice.6
  1.4 0.7 convert_bitcast_fusion
  2.1 0.7 convert_reduce_fusion.1
  2.9 0.8 reshape.24
  4.0 0.9 copy-done.8
  4.9 0.9 copy-done.9
  5.9 0.9 copy-done.10
  6.8 0.8 copy-done.15
  7.6 0.8 copy-done.16
  8.3 35.6 %gather_rows.1 = (bf16[8,512,128]{2,1,0:T(8,128)(2,1)S(1)}, bf16[8,512,128]{2,1,0:T(8,128)(2,1)S(1)}, bf16[16,2,128,128]{3,2,1,0:T(8,128)(2,1)S(1)}, f32[4,8,512]{2,1,0:T(8,128)S(1)}, f32[16,8,128]{2,1,0:T(8,128)S(1)}) custom-call(bf16[128,1024]{1,0:T(8,128)(2,1)S(1)} %bitcast.15, bf16[128,1024]{1,0:T(8,128)(2,1)S(1)} %bitcast.16, ...), custom_call_target="tpu_custom_call" | custom-call | tf_op jit(solution)/shard_map/gather_rows/pallas_call | solution.py:138
  44.0 1.0 copy-done.3
  45.0 8.2 %softmax_totals.1.part_ref = f32[2,8,512]{2,1,0:T(8,128)S(1)} custom-call(s32[40]{0:T(128)S(1)} %convert_reduce_fusion.meta_ref, bf16[8,512,128]{2,1,0:T(8,128)(2,1)S(1)} %get-tuple-element.19.qg_ref, bf16[16,2,128,128]{3,2,1,0:T(8,128)(2,1)S(1)} %get-tuple-element.21.kvg_ref, f32[4,8,512]{2,1,0:T(8,128)S(1)} %get-tuple-element.22.auxg_ref, ...), custom_call_target="tpu_custom_call" | custom-call | tf_op jit(solution)/shard_map/softmax_totals/pallas_call | solution.py:254
  53.2 0.6 copy-done.11
  53.8 6.1 %combine_totals.1.log_ref = f32[8,512]{1,0:T(8,128)} custom-call(f32[2,8,512]{2,1,0:T(8,128)} %copy-done.11), custom_call_target="tpu_custom_call" | custom-call | tf_op jit(solution)/shard_map/combine_totals/pallas_call | solution.py:295
  60.0 15.1 %attention_grads.1 = (bf16[8,512,128]{2,1,0:T(8,128)(2,1)}, bf16[16,128,256]{2,1,0:T(8,128)(2,1)}) custom-call(s32[40]{0:T(128)} %copy-done.17, bf16[8,512,128]{2,1,0:T(8,128)(2,1)} %copy-done, bf16[8,512,128]{2,1,0:T(8,128)(2,1)} %copy-done.3, bf16[16,2,128,128]{3,2,1,0:T(8,128)(2,1)} %copy-done.1, f32[4,8,512]{2,1,0:T(8,128)} %copy-done.6, ...), custom_call_target="tpu_custom_call" | custom-call | tf_op jit(solution)/shard_map/attention_grads/pallas_call | solution.py:373
  75.1 1.2 copy-done.4
  76.4 1.2 copy-done.5
  77.6 117.2 %reduce_and_update.1 = (bf16[128,1024]{1,0:T(8,128)(2,1)S(1)}, bf16[128,256]{1,0:T(8,128)(2,1)S(1)}, f32[2,32,128]{2,1,0:T(8,128)S(1)}, f32[2,32,128]{2,1,0:T(8,...) custom-call(bf16[16,128,256]{2,1,0:T(8,128)(2,1)S(1)} %copy-done.5, bf16[8,512,128]{2,1,0:T(8,128)(2,1)S(1)} %copy-done.4, ...), custom_call_target="tpu_custom_call" | custom-call | tf_op jit(solution)/shard_map/reduce_and_update/pallas_call | solution.py:578
  194.8 0.6 slice_reduce_fusion
  195.4 0.7 copy.22
  196.1 0.6 copy.23
  196.8 0.6 copy.24
  197.4 0.6 copy.25
  198.0 0.6 copy.26
  (35 shorter events, 0.5 us)
Async XLA Ops:
  4.0 1.0 copy-start.8
  4.9 0.9 copy-start.9
  5.9 0.9 copy-start.10
  6.8 0.8 copy-start.15
  7.6 0.8 copy-start.16
  8.3 51.6 %copy-start.17 = (s32[40]{0:T(128)}, s32[40]{0:T(128)S(1)}, u32[]{:S(2)}) copy-start(s32[40]{0:T(128)S(1)} %convert_reduce_fusion.meta_ref) | copy-start | bytes 484
  44.0 1.0 copy-start.3
  45.0 15.0 %copy-start = (bf16[8,512,128]{2,1,0:T(8,128)(2,1)}, bf16[8,512,128]{2,1,0:T(8,128)(2,1)S(1)}, u32[]{:S(2)}) copy-start(bf16[8,512,128]{2,1,0:T(8,128)(2,1)S(1)} %get-tuple-element.19.qg_ref) | copy-start | bytes 3145732
  45.0 15.0 %copy-start.1 = (bf16[16,2,128,128]{3,2,1,0:T(8,128)(2,1)}, bf16[16,2,128,128]{3,2,1,0:T(8,128)(2,1)S(1)}, u32[]{:S(2)}) copy-start(bf16[16,2,128,128]{3,2,1,0:T(8,128)(2,1)S(1)} %get-tuple-element.21.kvg_ref) | copy-start | bytes 3145732
  45.0 15.0 %copy-start.6 = (f32[4,8,512]{2,1,0:T(8,128)}, f32[4,8,512]{2,1,0:T(8,128)S(1)}, u32[]{:S(2)}) copy-start(f32[4,8,512]{2,1,0:T(8,128)S(1)} %get-tuple-element.22.auxg_ref) | copy-start | bytes 196612
  45.0 15.0 %copy-start.7 = (f32[16,8,128]{2,1,0:T(8,128)}, f32[16,8,128]{2,1,0:T(8,128)S(1)}, u32[]{:S(2)}) copy-start(f32[16,8,128]{2,1,0:T(8,128)S(1)} %get-tuple-element.23.segg_ref) | copy-start | bytes 196612
  53.2 0.6 copy-start.11
  53.8 21.3 %copy-start.12 = (f32[2,32,128]{2,1,0:T(8,128)S(1)}, f32[2,32,128]{2,1,0:T(8,128)}, u32[]{:S(2)}) copy-start(f32[2,32,128]{2,1,0:T(8,128)} %w_ref.1) | copy-start | bytes 98308
  53.8 21.3 %copy-start.13 = (f32[2,32,128]{2,1,0:T(8,128)S(1)}, f32[2,32,128]{2,1,0:T(8,128)}, u32[]{:S(2)}) copy-start(f32[2,32,128]{2,1,0:T(8,128)} %m1_ref.1) | copy-start | bytes 98308
  53.8 21.3 %copy-start.14 = (f32[2,32,128]{2,1,0:T(8,128)S(1)}, f32[2,32,128]{2,1,0:T(8,128)}, u32[]{:S(2)}) copy-start(f32[2,32,128]{2,1,0:T(8,128)} %m2_ref.1) | copy-start | bytes 98308
  60.0 15.1 %copy-start.2 = (bf16[1,128,8192]{2,1,0:T(8,128)(2,1)S(1)}, bf16[1,128,8192]{2,1,0:T(8,128)(2,1)}, u32[]{:S(2)}) copy-start(bf16[1,128,8192]{2,1,0:T(8,128)(2,1)} %param.16) | copy-start | bytes 6291460
  75.1 1.2 copy-start.4
  76.4 1.2 copy-start.5

commit v2 on v1

v2 whole, which is shorter than its diff:
```python
import functools

import jax
import jax.numpy as jnp
from jax import lax
from jax.experimental import pallas as pl
from jax.experimental.pallas import tpu as pltpu
from jax.sharding import PartitionSpec as P

beta_one = 0.9
beta_two = 0.999
epsilon = 1e-06
weight_decay = 0.01
learn_rate = 0.01

HEADS = 8
DIM = 128
SPAN = 64
ROWS = 128
LANES = HEADS * SPAN
BLOCK = 256
KEYS = 2048
EARLY = 8
SHIFTS = (1, 15, 2, 14, 3, 13, 4, 12, 5, 11, 6, 10, 7, 9, 8)
CHUNK = 512
VMEM_LIMIT = 62 * 1024 * 1024
SCALE = DIM ** (-0.5)
LOG2E = 1.4426950408889634
MESH = pl.DeviceIdType.MESH
VMEM = pltpu.VMEM
F32 = jnp.float32
BF16 = jnp.bfloat16


def vmem_spec():
    return pl.BlockSpec(memory_space=pltpu.VMEM)


def any_spec():
    return pl.BlockSpec(memory_space=pl.ANY)


def smem_spec():
    return pl.BlockSpec(memory_space=pltpu.SMEM)


def greet(peers):
    barrier = pltpu.get_barrier_semaphore()
    for peer in peers:
        pl.semaphore_signal(barrier, inc=1, device_id=peer, device_id_type=MESH)
    return barrier


def send(src, dst, send_sem, recv_sem, peer):
    copy = pltpu.make_async_remote_copy(
        src_ref=src, dst_ref=dst, send_sem=send_sem, recv_sem=recv_sem,
        device_id=peer, device_id_type=MESH,
    )
    copy.start()
    return copy


def arrived(dst, sem):
    pltpu.make_async_copy(dst, dst, sem).wait()


def place():
    me = lax.axis_index("context")
    dp = lax.axis_index("dp")
    return me, dp, me // 16, me % 16


def x_peers(me, dp, x, rest):
    return [(lax.rem(x + i, 4) * 16 + rest, dp) for i in range(1, 4)]


def rest_peers(me, dp, x, rest):
    return [(x * 16 + lax.rem(rest + i, 16), dp) for i in range(1, 16)]


def column_peers(me, dp):
    x, y_lo, z = me // 16, me // 8 % 2, me % 8
    y_hi, core = dp // 2, dp % 2
    column = x * 4 + y_lo * 2 + y_hi
    peers = []
    for shift in SHIFTS:
        there = lax.rem(column + shift, 16)
        peers.append(((there // 4) * 16 + (there // 2 % 2) * 8 + z, (there % 2) * 2 + core))
    return column, peers


def act_piece(act_ref, index):
    there = lax.rem(index, 16)
    return act_ref.at[:, pl.ds(pl.multiple_of(there * LANES, LANES), LANES)]


def gather_kernel(
    q_ref, g_ref, o_ref, k_ref, v_ref, act_ref, segk_ref, rows_ref, local_ref,
    qg_ref, kg_ref, auxg_ref, segg_ref, log_ref, gg_ref, vg_ref, actg_ref,
    q_own, g_own, o_own, gbuf, k_aug, q_aug, scores, part, got,
    x_send, x_recv, r_send, r_recv, act_send, act_recv, m_send, m_recv, own_sem,
):
    me, dp, x, rest = place()
    xs = x_peers(me, dp, x, rest)
    rs = rest_peers(me, dp, x, rest)
    column, columns = column_peers(me, dp)
    two = pl.ds(pl.multiple_of(2 * x, 2), 2)
    own = [
        pltpu.make_async_copy(k_ref, kg_ref.at[rest], own_sem.at[0]),
        pltpu.make_async_copy(segk_ref, segg_ref.at[rest], own_sem.at[1]),
        pltpu.make_async_copy(q_ref, q_own, own_sem.at[2]),
        pltpu.make_async_copy(g_ref, g_own, own_sem.at[3]),
        pltpu.make_async_copy(o_ref, o_own, own_sem.at[4]),
        pltpu.make_async_copy(v_ref, vg_ref.at[rest], own_sem.at[5]),
        pltpu.make_async_copy(rows_ref, auxg_ref.at[x], own_sem.at[6]),
    ]
    for copy in own:
        copy.start()
    barrier = greet(
        rs + [(lax.rem(me + i * 16, 64) // 16 * 16 + j * 8 + me % 8, k * 2 + dp % 2)
              for i in range(1, 4) for j in range(2) for k in range(2)]
        + [(x * 16 + j * 8 + me % 8, (1 - dp // 2) * 2 + dp % 2) for j in range(2)]
    )
    for copy in own:
        copy.wait()
    for span in range(2):
        rows = pl.ds(span * SPAN, SPAN)
        pieces = []
        for h in range(HEADS):
            cols = pl.ds(h * DIM, DIM)
            qg_ref[2 * x + span, pl.ds(h * SPAN, SPAN), :] = q_own[rows, cols]
            grad = g_own[rows, cols]
            gbuf[span, pl.ds(h * SPAN, SPAN), :] = grad
            pieces.append(grad.astype(F32) * o_own[rows, cols].astype(F32))
        product = jnp.concatenate(pieces, axis=0)
        auxg_ref[x, pl.ds(span, 1), :] = jnp.sum(product.T, axis=0, keepdims=True)
    pl.semaphore_wait(barrier, 15 + 12 + 2)

    copies = []
    for i, peer in enumerate(rs):
        if i < 3:
            copies.append(send(qg_ref.at[two], qg_ref.at[two], x_send.at[0, i], x_recv.at[0, x], xs[i]))
            copies.append(send(auxg_ref.at[x], auxg_ref.at[x], x_send.at[2, i], x_recv.at[2, x], xs[i]))
        copies.append(send(kg_ref.at[rest], kg_ref.at[rest], r_send.at[0, i], r_recv.at[0, rest], peer))
        copies.append(send(segk_ref, segg_ref.at[rest], r_send.at[1, i], r_recv.at[1, rest], peer))
    for i, peer in enumerate(rs):
        if i < 3:
            copies.append(send(gbuf, gg_ref.at[two], x_send.at[1, i], x_recv.at[1, x], xs[i]))
        copies.append(send(v_ref, vg_ref.at[rest], r_send.at[2, i], r_recv.at[2, rest], peer))
    own = pltpu.make_async_copy(gbuf, gg_ref.at[two], own_sem.at[3])
    own.start()
    for i in range(EARLY):
        copies.append(
            send(act_piece(act_ref, column + SHIFTS[i]), actg_ref.at[i], act_send.at[i],
                 act_recv.at[i], columns[i])
        )
    own.wait()

    for i in range(1, 16):
        slot = lax.rem(rest + i, 16)
        arrived(kg_ref.at[slot], r_recv.at[0, slot])
        arrived(segg_ref.at[slot], r_recv.at[1, slot])
    feature = lax.broadcasted_iota(jnp.int32, (DIM, ROWS), 0)
    half = lax.broadcasted_iota(jnp.int32, (DIM, ROWS), 1) // SPAN

    def key_step(slot, carry):
        seg = segg_ref[slot, pl.ds(0, 1), :].astype(jnp.int32)
        hot = (feature == seg) | (feature == 2 * slot + half + 4)
        rows = pl.ds(pl.multiple_of(slot * ROWS, ROWS), ROWS)
        k_aug[rows, pl.ds(0, DIM)] = kg_ref[slot]
        k_aug[rows, pl.ds(DIM, DIM)] = hot.astype(F32).T.astype(BF16)
        return carry

    lax.fori_loop(0, 16, key_step, 0)
    for i in range(1, 4):
        slot = lax.rem(x + i, 4)
        pair = pl.ds(2 * slot, 2)
        arrived(qg_ref.at[pair], x_recv.at[0, slot])
        arrived(auxg_ref.at[slot], x_recv.at[2, slot])

    document = lax.broadcasted_iota(jnp.int32, (DIM, LANES), 0)
    local = jnp.broadcast_to(local_ref[...], (DIM, LANES))

    def span_step(s, carry):
        slot = s // 2
        seg = auxg_ref[slot, pl.ds(2 + s % 2, 1), :].astype(jnp.int32)
        span = auxg_ref[slot, pl.ds(4 + s % 2, 1), :]
        unseen = ((document < 4) & (document != seg)) | (local > span)
        q_aug[pl.ds(0, DIM), :] = qg_ref[s].T
        q_aug[pl.ds(DIM, DIM), :] = jnp.where(unseen, -1e30, 0.0).astype(BF16)
        for c in range(0, KEYS, CHUNK):
            scores[pl.ds(c, CHUNK), :] = jnp.dot(
                k_aug[pl.ds(c, CHUNK), :], q_aug[...], preferred_element_type=F32
            )

        @pl.when(slot == x)
        def _():
            rows = pl.ds(pl.multiple_of(rest * ROWS + s % 2 * SPAN, SPAN), SPAN)
            later = lax.broadcasted_iota(jnp.int32, (SPAN, LANES), 0) > (
                lax.broadcasted_iota(jnp.int32, (SPAN, LANES), 1) % SPAN
            )
            scores[rows, :] = jnp.where(later, -1e30, scores[rows, :])

        top = jnp.max(scores[...], axis=0, keepdims=True)
        weights = jnp.exp2((scores[...] - top) * (SCALE * LOG2E))
        part[0, pl.ds(s, 1), :] = top
        part[1, pl.ds(s, 1), :] = jnp.sum(weights, axis=0, keepdims=True)
        return carry

    lax.fori_loop(0, 8, span_step, 0)
    got[x] = part[...]
    for i, peer in enumerate(xs):
        copies.append(send(part, got.at[x], m_send.at[i], m_recv.at[x], peer))
    for i in range(1, 4):
        slot = lax.rem(x + i, 4)
        arrived(got.at[slot], m_recv.at[slot])
    top = jnp.maximum(
        jnp.maximum(got[0, 0], got[1, 0]), jnp.maximum(got[2, 0], got[3, 0])
    )
    total = jnp.zeros_like(top)
    for slot in range(4):
        total = total + got[slot, 1] * jnp.exp2((got[slot, 0] - top) * (SCALE * LOG2E))
    log_ref[...] = top * (SCALE * LOG2E) + jnp.log(total) * LOG2E

    for i in range(1, 16):
        slot = lax.rem(rest + i, 16)
        arrived(vg_ref.at[slot], r_recv.at[2, slot])
    for i in range(1, 4):
        slot = lax.rem(x + i, 4)
        arrived(gg_ref.at[pl.ds(2 * slot, 2)], x_recv.at[1, slot])
    for i in range(EARLY):
        arrived(actg_ref.at[i], act_recv.at[i])
    for copy in copies:
        copy.wait_send()


def gather(queries, out_grad, attn_out, key_states, value_states, act, seg_keys, rows, local):
    dma = pltpu.SemaphoreType.DMA
    return pl.pallas_call(
        gather_kernel,
        out_shape=(
            jax.ShapeDtypeStruct((8, LANES, DIM), BF16),
            jax.ShapeDtypeStruct((16, ROWS, DIM), BF16),
            jax.ShapeDtypeStruct((4, 8, LANES), F32),
            jax.ShapeDtypeStruct((16, 8, ROWS), F32),
            jax.ShapeDtypeStruct((8, LANES), F32),
            jax.ShapeDtypeStruct((8, LANES, DIM), BF16),
            jax.ShapeDtypeStruct((16, ROWS, DIM), BF16),
            jax.ShapeDtypeStruct((EARLY, ROWS, LANES), BF16),
        ),
        in_specs=[any_spec()] * 8 + [vmem_spec()],
        out_specs=(vmem_spec(),) * 5 + (any_spec(),) * 3,
        scratch_shapes=[
            VMEM((ROWS, HEADS * DIM), BF16),
            VMEM((ROWS, HEADS * DIM), BF16),
            VMEM((ROWS, HEADS * DIM), BF16),
            VMEM((2, LANES, DIM), BF16),
            VMEM((KEYS, 2 * DIM), BF16),
            VMEM((2 * DIM, LANES), BF16),
            VMEM((KEYS, LANES), F32),
            VMEM((2, 8, LANES), F32),
            VMEM((4, 2, 8, LANES), F32),
            dma((3, 3)), dma((3, 4)),
            dma((3, 15)), dma((3, 16)),
            dma((EARLY,)), dma((EARLY,)),
            dma((3,)), dma((4,)),
            dma((7,)),
        ],
        compiler_params=pltpu.CompilerParams(
            collective_id=0, has_side_effects=True, vmem_limit_bytes=VMEM_LIMIT
        ),
        name="gather_and_totals",
    )(queries, out_grad, attn_out, key_states, value_states, act, seg_keys, rows, local)


def key_counts(segg_ref):
    seg = segg_ref[:, 0, :]
    return [jnp.sum((seg < d - 0.5).astype(F32)).astype(jnp.int32) for d in (1, 2, 3)]


def span_range(meta_ref, auxg_ref, counts, s):
    slot = s // 2
    seg = auxg_ref[slot, pl.ds(2 + s % 2, 1), :]
    low = jnp.where(
        seg > 2.5, counts[2], jnp.where(seg > 1.5, counts[1], jnp.where(seg > 0.5, counts[0], 0))
    )
    x = lax.axis_index("context") // 16
    own = (slot == x).astype(jnp.int32)
    base = meta_ref[32 + s] * SPAN
    row = lax.broadcasted_iota(jnp.int32, (1, LANES), 1) % SPAN
    high = base + own * (row + 1)
    low_min, low_max = jnp.min(low), jnp.max(low)
    high_min, high_max = base + own, base + own * SPAN
    first = low_min // BLOCK
    last = (high_max + BLOCK - 1) // BLOCK
    return low, high, low_max, high_min, first, last


def inside(low, high, block):
    place_of = block * BLOCK + lax.broadcasted_iota(jnp.int32, (BLOCK, LANES), 0)
    return (place_of >= low) & (place_of < high)


def sort_keys(meta_ref, stored_ref, sorted_ref):
    def step(t, carry):
        rank = meta_ref[t]
        source = pl.multiple_of((t % 2) * SPAN, SPAN)
        target = pl.multiple_of(rank * SPAN, SPAN)
        sorted_ref[pl.ds(target, SPAN), :] = stored_ref[t // 2, pl.ds(source, SPAN), :]
        return carry

    lax.fori_loop(0, 32, step, 0)


def grads_kernel(
    meta_ref, qg_ref, gg_ref, kg_ref, vg_ref, auxg_ref, segg_ref, log_ref,
    dq_ref, dkv_ref,
    ks, vs, kt, qt, gt, dqt, dk, dv,
):
    sort_keys(meta_ref, kg_ref, ks)
    sort_keys(meta_ref, vg_ref, vs)
    for b in range(KEYS // BLOCK):
        kt[b] = ks[pl.ds(b * BLOCK, BLOCK), :].T
    dk[...] = jnp.zeros_like(dk)
    dv[...] = jnp.zeros_like(dv)
    counts = key_counts(segg_ref)

    def span_step(s, carry):
        low, high, low_max, high_min, first, last = span_range(meta_ref, auxg_ref, counts, s)
        qt[...] = qg_ref[s].T
        gt[...] = gg_ref[s].T
        dqt[...] = jnp.zeros_like(dqt)
        log_total = log_ref[pl.ds(s, 1), :]
        delta = auxg_ref[s // 2, pl.ds(s % 2, 1), :]

        def tile(block, masked):
            rows = pl.ds(pl.multiple_of(block * BLOCK, BLOCK), BLOCK)
            scores = jnp.dot(ks[rows, :], qt[...], preferred_element_type=F32)
            probs = jnp.exp2(scores * (SCALE * LOG2E) - log_total)
            if masked:
                probs = jnp.where(inside(low, high, block), probs, 0.0)
            prob_grad = jnp.dot(vs[rows, :], gt[...], preferred_element_type=F32)
            score_grad = (SCALE * probs * (prob_grad - delta)).astype(BF16)
            dv[rows, :] += jnp.dot(probs.astype(BF16), gg_ref[s], preferred_element_type=F32)
            dk[rows, :] += jnp.dot(score_grad, qg_ref[s], preferred_element_type=F32)
            dqt[...] += jnp.dot(kt[block], score_grad, preferred_element_type=F32)

        def block_step(block, carry):
            edge = (block * BLOCK < low_max) | ((block + 1) * BLOCK > high_min)

            @pl.when(edge)
            def _():
                tile(block, True)

            @pl.when(jnp.logical_not(edge))
            def _():
                tile(block, False)

            return carry

        lax.fori_loop(first, last, block_step, 0)
        dq_ref[s] = dqt[...].T.astype(BF16)
        return carry

    lax.fori_loop(0, 8, span_step, 0)

    def unsort(t, carry):
        source = pl.ds(pl.multiple_of(meta_ref[t] * SPAN, SPAN), SPAN)
        target = pl.ds(pl.multiple_of((t % 2) * SPAN, SPAN), SPAN)
        dkv_ref[0, t // 2, target, :] = dk[source, :].astype(BF16)
        dkv_ref[1, t // 2, target, :] = dv[source, :].astype(BF16)
        return carry

    lax.fori_loop(0, 32, unsort, 0)


def grads(meta, qg, gg, kg, vg, auxg, segg, log_total):
    return pl.pallas_call(
        grads_kernel,
        out_shape=(
            jax.ShapeDtypeStruct((8, LANES, DIM), BF16),
            jax.ShapeDtypeStruct((2, 16, ROWS, DIM), BF16),
        ),
        in_specs=[smem_spec()] + [vmem_spec()] * 7,
        out_specs=(vmem_spec(),) * 2,
        scratch_shapes=[
            VMEM((KEYS, DIM), BF16),
            VMEM((KEYS, DIM), BF16),
            VMEM((KEYS // BLOCK, DIM, BLOCK), BF16),
            VMEM((DIM, LANES), BF16),
            VMEM((DIM, LANES), BF16),
            VMEM((DIM, LANES), F32),
            VMEM((KEYS, DIM), F32),
            VMEM((KEYS, DIM), F32),
        ],
        compiler_params=pltpu.CompilerParams(vmem_limit_bytes=VMEM_LIMIT),
        name="attention_grads",
    )(meta, qg, gg, kg, vg, auxg, segg, log_total)


def tail_kernel(
    dkv_ref, dq_ref, act_ref, actg_ref, w_ref, m1_ref, m2_ref,
    qgrad_ref, kvgrad_ref, nw_ref, n1_ref, n2_ref, trust_ref,
    dkv_in, dq_in, act_in, kv_in, partial, g_in, a_in, a_msg, b_in, b_msg,
    r_send, r_recv, x_send, x_recv, act_send, act_recv, kv_send, kv_recv,
    g_send, g_recv, a_send, a_recv, b_send, b_recv, own_sem,
):
    me, dp, x, rest = place()
    y_lo, z = rest // 8, rest % 8
    y_hi, core = dp // 2, dp % 2
    line = z * 2 + core
    xs = x_peers(me, dp, x, rest)
    rs = rest_peers(me, dp, x, rest)
    column, columns = column_peers(me, dp)

    def in_line(index):
        return (x * 16 + y_lo * 8 + index // 2, y_hi * 2 + index % 2)

    lines = [in_line(lax.rem(line + i, 16)) for i in range(1, 16)]
    greeted = [
        (x * 16 + y_lo * 8 + lax.rem(z + i // 4, 8), lax.rem(dp + i % 4, 4)) for i in range(1, 32)
    ]
    greeted += [(x * 16 + (1 - y_lo) * 8 + i, dp) for i in range(8)]
    greeted += [
        (lax.rem(x + i, 4) * 16 + j * 8 + z, k * 2 + core)
        for i in range(1, 4) for j in range(2) for k in range(2)
    ]
    greeted += [(x * 16 + (1 - y_lo) * 8 + z, (1 - y_hi) * 2 + core)]
    barrier = greet(greeted)
    own = [
        pltpu.make_async_copy(dkv_ref.at[:, rest], dkv_in.at[:, rest], own_sem.at[0]),
        pltpu.make_async_copy(dq_ref.at[pl.ds(2 * x, 2)], dq_in.at[x], own_sem.at[1]),
        pltpu.make_async_copy(act_piece(act_ref, column), act_in.at[0], own_sem.at[2]),
        pltpu.make_async_copy(actg_ref, act_in.at[pl.ds(1, EARLY)], own_sem.at[3]),
    ]
    for copy in own:
        copy.start()
    pl.semaphore_wait(barrier, len(greeted))

    copies = []
    for p in range(2):
        for i, peer in enumerate(rs):
            there = lax.rem(rest + i + 1, 16)
            copies.append(
                send(dkv_ref.at[p, there], dkv_in.at[p, rest], r_send.at[p, i],
                     r_recv.at[p, rest], peer)
            )
    for i in range(EARLY, 15):
        copies.append(
            send(act_piece(act_ref, column + SHIFTS[i]), act_in.at[i + 1], act_send.at[i],
                 act_recv.at[i], columns[i])
        )
    for copy in own:
        copy.wait()

    for p in range(2):
        for i in range(1, 16):
            slot = lax.rem(rest + i, 16)
            arrived(dkv_in.at[p, slot], r_recv.at[p, slot])
        summed = dkv_in[p, 0].astype(F32)
        for slot in range(1, 16):
            summed = summed + dkv_in[p, slot].astype(F32)
        kv_low = summed.astype(BF16)
        kv_in[p, 0] = kv_low
        kvgrad_ref[:, pl.ds(p * DIM, DIM)] = kv_low
        for i, peer in enumerate(columns):
            copies.append(
                send(kv_in.at[p, 0], kv_in.at[p, i + 1], kv_send.at[p, i], kv_recv.at[p, i], peer)
            )
    for i, peer in enumerate(xs):
        there = lax.rem(x + i + 1, 4)
        copies.append(
            send(dq_ref.at[pl.ds(2 * there, 2)], dq_in.at[x], x_send.at[i], x_recv.at[x], peer)
        )

    here = z // 4 == y_hi

    def to_owner(p, i):
        there_z = lax.rem(z % 4 + i // 4, 4)
        there_dp = lax.rem(dp + i % 4, 4)
        rows = pl.ds(pl.multiple_of((there_z * 4 + there_dp) * 32, 32), 32)
        return pltpu.make_async_remote_copy(
            src_ref=partial.at[p, rows], dst_ref=g_in.at[p, line], send_sem=g_send.at[p, i],
            recv_sem=g_recv.at[p, line],
            device_id=(x * 16 + y_lo * 8 + y_hi * 4 + there_z, there_dp), device_id_type=MESH,
        )

    own_rows = pl.ds(pl.multiple_of((z % 4 * 4 + dp) * 32, 32), 32)
    for i in range(EARLY, 15):
        arrived(act_in.at[i + 1], act_recv.at[i])
    for p in range(2):
        total = jnp.zeros((DIM, LANES), F32)
        for i in range(16):
            if i > 0:
                arrived(kv_in.at[p, i], kv_recv.at[p, i - 1])
            total = total + jnp.dot(kv_in[p, i].T, act_in[i], preferred_element_type=F32)
        partial[p] = total.T.astype(BF16)
        for i in range(1, 16):
            to_owner(p, i).start()

        @pl.when(here)
        def _():
            pltpu.make_async_copy(
                partial.at[p, own_rows], g_in.at[p, line], g_recv.at[p, line]
            ).start()

        @pl.when(jnp.logical_not(here))
        def _():
            to_owner(p, 0).start()

    sums, updates = [], []
    for p in range(2):
        for slot in range(16):
            arrived(g_in.at[p, slot], g_recv.at[p, slot])
        grad = g_in[p, 0].astype(F32)
        for slot in range(1, 16):
            grad = grad + g_in[p, slot].astype(F32)
        weight = w_ref[p]
        one = beta_one * m1_ref[p] + (1.0 - beta_one) * grad
        two = beta_two * m2_ref[p] + (1.0 - beta_two) * grad * grad
        n1_ref[p] = one
        n2_ref[p] = two
        update = one / (jnp.sqrt(two) + epsilon) + weight_decay * weight
        updates.append(update)
        sums.append(jnp.sum(weight * weight, axis=0, keepdims=True))
        sums.append(jnp.sum(update * update, axis=0, keepdims=True))
    a_msg[...] = jnp.concatenate(sums + [jnp.zeros((4, DIM), F32)], axis=0)
    a_in[column] = a_msg[...]
    for i, peer in enumerate(columns):
        copies.append(send(a_msg, a_in.at[column], a_send.at[i], a_recv.at[column], peer))

    for i in range(1, 4):
        slot = lax.rem(x + i, 4)
        arrived(dq_in.at[slot], x_recv.at[slot])
    for span in range(2):
        for h in range(HEADS):
            rows = pl.ds(h * SPAN, SPAN)
            summed = dq_in[0, span, rows, :].astype(F32)
            for slot in range(1, 4):
                summed = summed + dq_in[slot, span, rows, :].astype(F32)
            qgrad_ref[pl.ds(span * SPAN, SPAN), pl.ds(h * DIM, DIM)] = summed.astype(BF16)

    for i in range(1, 16):
        slot = lax.rem(column + i, 16)
        arrived(a_in.at[slot], a_recv.at[slot])
    summed = a_in[0]
    for slot in range(1, 16):
        summed = summed + a_in[slot]
    b_msg[...] = summed
    b_in[line] = summed
    late = [
        send(b_msg, b_in.at[line], b_send.at[i], b_recv.at[line], peer)
        for i, peer in enumerate(lines)
    ]
    for copy in copies:
        copy.wait_send()
    for p in range(2):
        for i in range(1, 16):
            to_owner(p, i).wait_send()

        @pl.when(jnp.logical_not(here))
        def _():
            to_owner(p, 0).wait_send()

    for i in range(1, 16):
        slot = lax.rem(line + i, 16)
        arrived(b_in.at[slot], b_recv.at[slot])
    summed = b_in[0]
    for slot in range(1, 16):
        summed = summed + b_in[slot]
    norms = jnp.sqrt(jnp.sum(summed, axis=1, keepdims=True))
    ratios = []
    for p in range(2):
        ratio = norms[2 * p:2 * p + 1] / (norms[2 * p + 1:2 * p + 2] + epsilon)
        ratios.append(ratio)
        nw_ref[p] = w_ref[p] - learn_rate * ratio * updates[p]
    trust_ref[...] = jnp.concatenate(
        [jnp.broadcast_to(ratio, (1, DIM)) for ratio in ratios] + [jnp.zeros((6, DIM), F32)], axis=0
    )
    for copy in late:
        copy.wait_send()


def tail(dkv, dq, act, actg, kv_weight, moment_one, moment_two):
    state = jax.ShapeDtypeStruct((2, 32, DIM), F32)
    dma = pltpu.SemaphoreType.DMA
    return pl.pallas_call(
        tail_kernel,
        out_shape=(
            jax.ShapeDtypeStruct((ROWS, HEADS * DIM), BF16),
            jax.ShapeDtypeStruct((ROWS, 2 * DIM), BF16),
            state, state, state,
            jax.ShapeDtypeStruct((8, DIM), F32),
        ),
        in_specs=[any_spec()] * 4 + [vmem_spec()] * 3,
        out_specs=(vmem_spec(),) * 6,
        scratch_shapes=[
            VMEM((2, 16, ROWS, DIM), BF16),
            VMEM((4, 2, LANES, DIM), BF16),
            VMEM((16, ROWS, LANES), BF16),
            VMEM((2, 16, ROWS, DIM), BF16),
            VMEM((2, LANES, DIM), BF16),
            VMEM((2, 16, 32, DIM), BF16),
            VMEM((16, 8, DIM), F32),
            VMEM((8, DIM), F32),
            VMEM((16, 8, DIM), F32),
            VMEM((8, DIM), F32),
            dma((2, 15)), dma((2, 16)),
            dma((3,)), dma((4,)),
            dma((15,)), dma((15,)),
            dma((2, 15)), dma((2, 15)),
            dma((2, 16)), dma((2, 16)),
            dma((15,)), dma((16,)),
            dma((15,)), dma((16,)),
            dma((4,)),
        ],
        compiler_params=pltpu.CompilerParams(
            collective_id=2, has_side_effects=True, vmem_limit_bytes=48 * 1024 * 1024
        ),
        name="reduce_and_update",
    )(dkv, dq, act, actg, kv_weight, moment_one, moment_two)


def on_device(
    queries,
    key_states,
    value_states,
    attn_out,
    out_grad,
    activations,
    segment_ids,
    span_order,
    kv_weight,
    moment_one,
    moment_two,
):
    me = lax.axis_index("context")
    x, rest = me // 16, me % 16
    local = lax.dynamic_slice_in_dim(span_order, x * 32, 32, 0)
    mine = lax.dynamic_slice_in_dim(span_order.reshape(4, 16, 2), rest, 1, 1).reshape(8)
    asked = jnp.concatenate([local, mine])
    meta = jnp.sum((local[None, :] < asked[:, None]).astype(jnp.int32), axis=1)
    seg = segment_ids.astype(F32).reshape(2, 1, SPAN)
    spans = lax.dynamic_slice_in_dim(span_order, 2 * me, 2, 0).astype(F32)
    rows = jnp.concatenate(
        [
            jnp.zeros((2, LANES), F32),
            jnp.tile(seg, (1, HEADS, 1)).reshape(2, LANES),
            jnp.broadcast_to(spans[:, None], (2, LANES)),
            jnp.zeros((2, LANES), F32),
        ]
    )
    seg_keys = jnp.broadcast_to(seg.reshape(1, ROWS), (8, ROWS))
    local_ids = jnp.pad(local.astype(F32), (4, DIM - 36), constant_values=-1.0)[:, None]
    qg, kg, auxg, segg, log_total, gg, vg, actg = gather(
        queries[0], out_grad[0], attn_out[0], key_states[0], value_states[0], activations[0],
        seg_keys, rows, local_ids,
    )
    dq, dkv = grads(meta, qg, gg, kg, vg, auxg, segg, log_total)
    query_grad, kv_grad, new_weight, new_one, new_two, trust = tail(
        dkv, dq, activations[0], actg, kv_weight, moment_one, moment_two
    )
    return (query_grad[None], kv_grad[None], new_weight, new_one, new_two, trust[:2, 0])


def solution(mesh):
    in_specs = (
        P("dp", "context", None),
        P("dp", "context", None),
        P("dp", "context", None),
        P("dp", "context", None),
        P("dp", "context", None),
        P("dp", "context", None),
        P("dp", "context"),
        P(),
        P(None, ("context", "dp"), None),
        P(None, ("context", "dp"), None),
        P(None, ("context", "dp"), None),
    )
    out_specs = (
        P("dp", "context", None),
        P("dp", "context", None),
        P(None, ("context", "dp"), None),
        P(None, ("context", "dp"), None),
        P(None, ("context", "dp"), None),
        P(),
    )
    return jax.shard_map(
        on_device, mesh=mesh, in_specs=in_specs, out_specs=out_specs, check_vma=False
    )
```

time: 199 us -> 156 us (0.78)
  Pallas kernels: 182 us -> 141 us
  local copies, waits for them, and re-layouts: 14.1 us -> 10.4 us
  other arithmetic: 1.5 us -> 4.15 us
    pallas_call x1, Pallas kernels: 117 us -> 73.7 us  [tail(): pl.pallas_call(tail_kernel, out_shape=(jax.ShapeDtypeStruct((ROWS, HEADS...]
    pallas_call x2 -> x0, Pallas kernels: 14.3 us -> none  [the longest x1 8.21 us: stats(): pl.pallas_call(stats_kernel, out_shape=jax.ShapeDtypeStruct((2, 8, LANES)...]
    pallas_call x1, Pallas kernels: 35.6 us -> 49.7 us  [gather(): pl.pallas_call(gather_kernel, out_shape=(jax.ShapeDtypeStruct((8, LANES,...]
    unnamed x41 -> x19, local copies, waits for them, and re-layouts: 11.6 us -> 7.23 us
    pallas_call x1, Pallas kernels: 15.1 us -> 17.2 us  [grads(): pl.pallas_call(grads_kernel, out_shape=(jax.ShapeDtypeStruct((8, LANES, D...]
where the time goes in v2:
time: 156 us
  Pallas kernels  141 us (90%)
  local copies, waits for them, and re-layouts  10.4 us (7%)
  other arithmetic  4.15 us (3%)
    pallas_call x1, Pallas kernels, tail(): pl.pallas_call(tail_kernel, out_shape=(jax.ShapeDtypeStruct((ROWS, HEADS...  73.7 us
    pallas_call x1, Pallas kernels, gather(): pl.pallas_call(gather_kernel, out_shape=(jax.ShapeDtypeStruct((8, LANES,...  49.7 us
    pallas_call x1, Pallas kernels, grads(): pl.pallas_call(grads_kernel, out_shape=(jax.ShapeDtypeStruct((8, LANES, D...  17.2 us
    unnamed x19, local copies, waits for them, and re-layouts  7.23 us

profile of v2, /device:TPU:1, one launch (start us, length us, event | category | flops | bytes accessed | tf_op | source)
XLA Modules:
  0.0 156.0 jit_solution(10209902714761474846)
XLA Ops:
  0.7 0.7 dynamic-slice_convert_fusion
  1.5 0.7 convert_reduce_fusion.1
  2.1 0.1 tile.9
  2.2 0.7 convert_bitcast_fusion
  2.9 0.7 fusion
  3.7 0.6 broadcast_in_dim.25.segk_ref
  4.3 0.1 tile.11
  4.4 0.7 pad_maximum_fusion.rows_ref
  5.0 0.8 reshape.25
  5.9 0.1 reshape.26
  6.0 0.6 convert_reduce_fusion.meta_ref
  6.6 0.7 copy.19.local_ref
  7.4 49.7 %gather_and_totals.1 = (bf16[8,512,128]{2,1,0:T(8,128)(2,1)}, bf16[16,128,128]{2,1,0:T(8,128)(2,1)}, f32[4,8,512]{2,1,0:T(8,128)}, f32[16,8,128]{2,1,0:T(8,128)}...) custom-call(bf16[128,1024]{1,0:T(8,128)(2,1)} %bitcast.20, ...), custom_call_target="tpu_custom_call" | custom-call | tf_op jit(solution)/shard_map/gather_and_totals/pallas_call | solution.py:239
  57.1 17.2 %attention_grads.1 = (bf16[8,512,128]{2,1,0:T(8,128)(2,1)}, bf16[2,16,128,128]{3,2,1,0:T(8,128)(2,1)}) custom-call(s32[40]{0:T(128)} %convert_reduce_fusion.meta_ref, bf16[8,512,128]{2,1,0:T(8,128)(2,1)} %get-tuple-element.22.qg_ref, bf16[8,512,128]{2,1,0:T(8,128)(2,1)} %get-tuple-element.23.gg_ref, bf16[16,128,128]{2,1,0:T(8,128)(2,1)} %get-tuple-element.24.kg_ref, ...), custom_call_target="tpu_custom_call" | custom-call | tf_op jit(solution)/shard_map/attention_grads/pallas_call | solution.py:378
  74.4 1.6 %copy-done = bf16[1,128,8192]{2,1,0:T(8,128)(2,1)S(1)} copy-done((bf16[1,128,8192]{2,1,0:T(8,128)(2,1)S(1)}, bf16[1,128,8192]{2,1,0:T(8,128)(2,1)}, u32[]{:S(2)}) %copy-start) | copy-done | bytes 2097176
  76.0 1.2 copy-done.2
  77.2 1.2 copy-done.3
  78.4 73.7 %reduce_and_update.1 = (bf16[128,1024]{1,0:T(8,128)(2,1)S(1)}, bf16[128,256]{1,0:T(8,128)(2,1)S(1)}, f32[2,32,128]{2,1,0:T(8,128)S(1)}, f32[2,32,128]{2,1,0:T(8,...) custom-call(bf16[2,16,128,128]{3,2,1,0:T(8,128)(2,1)S(1)} %copy-done.3, bf16[8,512,128]{2,1,0:T(8,128)(2,1)S(1)} %copy-done.2, ...), custom_call_target="tpu_custom_call" | custom-call | tf_op jit(solution)/shard_map/reduce_and_update/pallas_call | solution.py:587
  152.1 0.6 slice_reduce_fusion
  152.8 0.7 copy.25
  153.5 0.6 copy.26
  154.1 0.6 copy.27
  154.7 0.6 copy.28
  155.3 0.6 copy.29
  (17 shorter events, 0.3 us)
Async XLA Ops:
  57.0 17.3 %copy-start.1 = (bf16[8,128,512]{2,1,0:T(8,128)(2,1)S(1)}, bf16[8,128,512]{2,1,0:T(8,128)(2,1)}, u32[]{:S(2)}) copy-start(bf16[8,128,512]{2,1,0:T(8,128)(2,1)} %get-tuple-element.31.actg_ref) | copy-start | bytes 3145732
  57.1 17.3 %copy-start.4 = (f32[2,32,128]{2,1,0:T(8,128)S(1)}, f32[2,32,128]{2,1,0:T(8,128)}, u32[]{:S(2)}) copy-start(f32[2,32,128]{2,1,0:T(8,128)} %w_ref.1) | copy-start | bytes 98308
  57.1 17.3 %copy-start.5 = (f32[2,32,128]{2,1,0:T(8,128)S(1)}, f32[2,32,128]{2,1,0:T(8,128)}, u32[]{:S(2)}) copy-start(f32[2,32,128]{2,1,0:T(8,128)} %m1_ref.1) | copy-start | bytes 98308
  57.1 17.3 %copy-start.6 = (f32[2,32,128]{2,1,0:T(8,128)S(1)}, f32[2,32,128]{2,1,0:T(8,128)}, u32[]{:S(2)}) copy-start(f32[2,32,128]{2,1,0:T(8,128)} %m2_ref.1) | copy-start | bytes 98308
  74.4 1.6 %copy-start = (bf16[1,128,8192]{2,1,0:T(8,128)(2,1)S(1)}, bf16[1,128,8192]{2,1,0:T(8,128)(2,1)}, u32[]{:S(2)}) copy-start(bf16[1,128,8192]{2,1,0:T(8,128)(2,1)} %param.16) | copy-start | bytes 6291460
  76.0 1.2 copy-start.2
  77.2 1.2 copy-start.3

commit v3 on v0

v3 whole, which is shorter than its diff:
```python
import functools

import jax
import jax.numpy as jnp
from jax import lax
from jax.experimental import pallas as pl
from jax.experimental.pallas import tpu as pltpu
from jax.sharding import PartitionSpec as P

beta_one = 0.9
beta_two = 0.999
epsilon = 1e-06
weight_decay = 0.01
learn_rate = 0.01

HEADS = 8
DIM = 128
SPAN = 64
ROWS = 128
LANES = HEADS * SPAN
BLOCK = 256
KEYS = 2048
LOG_ROW = 48
SHIFTS = (1, 15, 2, 14, 3, 13, 4, 12, 5, 11, 6, 10, 7, 9, 8)
CHUNK = 512
VMEM_LIMIT = 62 * 1024 * 1024
SCALE = DIM ** (-0.5)
LOG2E = 1.4426950408889634
MESH = pl.DeviceIdType.MESH
VMEM = pltpu.VMEM
F32 = jnp.float32
BF16 = jnp.bfloat16


def vmem_spec():
    return pl.BlockSpec(memory_space=pltpu.VMEM)


def any_spec():
    return pl.BlockSpec(memory_space=pl.ANY)


def smem_spec():
    return pl.BlockSpec(memory_space=pltpu.SMEM)


def greet(peers):
    barrier = pltpu.get_barrier_semaphore()
    for peer in peers:
        pl.semaphore_signal(barrier, inc=1, device_id=peer, device_id_type=MESH)
    return barrier


def send(src, dst, send_sem, recv_sem, peer):
    copy = pltpu.make_async_remote_copy(
        src_ref=src, dst_ref=dst, send_sem=send_sem, recv_sem=recv_sem,
        device_id=peer, device_id_type=MESH,
    )
    copy.start()
    return copy


def arrived(dst, sem):
    pltpu.make_async_copy(dst, dst, sem).wait()


def place():
    me = lax.axis_index("context")
    dp = lax.axis_index("dp")
    return me, dp, me // 16, me % 16


def x_peers(me, dp, x, rest):
    return [(lax.rem(x + i, 4) * 16 + rest, dp) for i in range(1, 4)]


def rest_peers(me, dp, x, rest):
    return [(x * 16 + lax.rem(rest + i, 16), dp) for i in range(1, 16)]


def column_peers(me, dp):
    x, y_lo, z = me // 16, me // 8 % 2, me % 8
    y_hi, core = dp // 2, dp % 2
    column = x * 4 + y_lo * 2 + y_hi
    peers = []
    for shift in SHIFTS:
        there = lax.rem(column + shift, 16)
        peers.append(((there // 4) * 16 + (there // 2 % 2) * 8 + z, (there % 2) * 2 + core))
    return column, peers


def act_piece(act_ref, index):
    there = lax.rem(index, 16)
    return act_ref.at[:, pl.ds(pl.multiple_of(there * LANES, LANES), LANES)]


def pieces_of(value):
    first = value.astype(BF16)
    left = value - first.astype(F32)
    second = left.astype(BF16)
    third = (left - second.astype(F32)).astype(BF16)
    zeros = jnp.zeros((13, value.shape[1]), F32)
    return jnp.concatenate(
        [first.astype(F32), second.astype(F32), third.astype(F32), zeros], axis=0
    ).astype(BF16)


def whole_kernel(
    order_ref, q_ref, g_ref, o_ref, k_ref, v_ref, act_ref, seg_ref, w_ref, m1_ref, m2_ref,
    qgrad_ref, kvgrad_ref, update_ref, n1_ref, n2_ref, trust_ref,
    q_own, g_own, o_own, qg, gg, kg, vg, auxg, segg, k_aug, v_aug, q_aug, g_aug, kt,
    scores, part, got, dk_acc, dv_acc, dqt, dkv_out, dkv_in, dq_out, dq_in,
    act_in, kv_in, partial, g_in, a_in, a_msg, b_in, b_msg,
    x_send, x_recv, r_send, r_recv, act_send, act_recv, m_send, m_recv,
    d_send, d_recv, dq_send, dq_recv, kv_send, kv_recv,
    gr_send, gr_recv, a_send, a_recv, b_send, b_recv, own_sem,
):
    me, dp, x, rest = place()
    y_lo, z = rest // 8, rest % 8
    y_hi, core = dp // 2, dp % 2
    line = z * 2 + core
    xs = x_peers(me, dp, x, rest)
    rs = rest_peers(me, dp, x, rest)
    column, columns = column_peers(me, dp)
    two = pl.ds(pl.multiple_of(2 * x, 2), 2)

    def in_line(index):
        return (x * 16 + y_lo * 8 + index // 2, y_hi * 2 + index % 2)

    lines = [in_line(lax.rem(line + i, 16)) for i in range(1, 16)]
    own = [
        pltpu.make_async_copy(k_ref, kg.at[rest], own_sem.at[0]),
        pltpu.make_async_copy(q_ref, q_own, own_sem.at[2]),
        pltpu.make_async_copy(g_ref, g_own, own_sem.at[3]),
        pltpu.make_async_copy(o_ref, o_own, own_sem.at[4]),
        pltpu.make_async_copy(v_ref, vg.at[rest], own_sem.at[5]),
        pltpu.make_async_copy(act_piece(act_ref, column), act_in.at[0], own_sem.at[1]),
    ]
    for copy in own:
        copy.start()
    greeted = [
        (x * 16 + y_lo * 8 + lax.rem(z + i // 4, 8), lax.rem(dp + i % 4, 4)) for i in range(1, 32)
    ]
    greeted += [(x * 16 + (1 - y_lo) * 8 + i, dp) for i in range(8)]
    greeted += [
        (lax.rem(x + i, 4) * 16 + j * 8 + z, k * 2 + core)
        for i in range(1, 4) for j in range(2) for k in range(2)
    ]
    greeted += [(x * 16 + (1 - y_lo) * 8 + z, (1 - y_hi) * 2 + core)]
    barrier = greet(greeted)
    seg_own = jnp.broadcast_to(seg_ref[...], (8, ROWS)).astype(F32)
    segg[rest] = seg_own
    swapped = pltpu.roll(seg_own, SPAN, 1)
    lower = lax.broadcasted_iota(jnp.int32, (8, ROWS), 1) < SPAN
    row_of = lax.broadcasted_iota(jnp.int32, (8, LANES), 0)
    auxg[x] = jnp.where(
        row_of == 2, jnp.concatenate([jnp.where(lower, seg_own, swapped)] * 4, axis=1),
        jnp.where(
            row_of == 3, jnp.concatenate([jnp.where(lower, swapped, seg_own)] * 4, axis=1),
            jnp.where(row_of == 4, order_ref[2 * me], order_ref[2 * me + 1]).astype(F32),
        ),
    )
    span_row = lax.broadcasted_iota(jnp.int32, (DIM, DIM), 0)
    local = jnp.full((DIM, DIM), -1, jnp.int32)
    for t in range(32):
        local = jnp.where(span_row == t + 4, order_ref[32 * x + t], local)
    local = jnp.concatenate([local] * (LANES // DIM), axis=1).astype(F32)
    for copy in own:
        copy.wait()
    for span in range(2):
        rows = pl.ds(span * SPAN, SPAN)
        products = []
        for h in range(HEADS):
            cols = pl.ds(h * DIM, DIM)
            qg[2 * x + span, pl.ds(h * SPAN, SPAN), :] = q_own[rows, cols]
            grad = g_own[rows, cols]
            gg[2 * x + span, pl.ds(h * SPAN, SPAN), :] = grad
            products.append(grad.astype(F32) * o_own[rows, cols].astype(F32))
        product = jnp.concatenate(products, axis=0)
        auxg[x, pl.ds(span, 1), :] = jnp.sum(product.T, axis=0, keepdims=True)
    pl.semaphore_wait(barrier, len(greeted))

    copies = []
    for i, peer in enumerate(rs):
        if i < 3:
            copies.append(send(qg.at[two], qg.at[two], x_send.at[0, i], x_recv.at[0, x], xs[i]))
            copies.append(send(auxg.at[x], auxg.at[x], x_send.at[2, i], x_recv.at[2, x], xs[i]))
        copies.append(send(kg.at[rest], kg.at[rest], r_send.at[0, i], r_recv.at[0, rest], peer))
        copies.append(send(segg.at[rest], segg.at[rest], r_send.at[1, i], r_recv.at[1, rest], peer))
    for i, peer in enumerate(rs):
        if i < 3:
            copies.append(send(gg.at[two], gg.at[two], x_send.at[1, i], x_recv.at[1, x], xs[i]))
        copies.append(send(vg.at[rest], vg.at[rest], r_send.at[2, i], r_recv.at[2, rest], peer))
    for i in range(1, 16):
        slot = lax.rem(rest + i, 16)
        arrived(kg.at[slot], r_recv.at[0, slot])
        arrived(segg.at[slot], r_recv.at[1, slot])
    feature = lax.broadcasted_iota(jnp.int32, (DIM, ROWS), 0)
    half = lax.broadcasted_iota(jnp.int32, (DIM, ROWS), 1) // SPAN
    ones = (feature >= LOG_ROW) & (feature < LOG_ROW + 3)

    def key_step(slot, carry):
        seg = segg[slot, pl.ds(0, 1), :].astype(jnp.int32)
        hot = (feature == seg) | (feature == 2 * slot + half + 4) | ones
        rows = pl.ds(pl.multiple_of(slot * ROWS, ROWS), ROWS)
        k_aug[rows, pl.ds(0, DIM)] = kg[slot]
        k_aug[rows, pl.ds(DIM, DIM)] = hot.astype(F32).T.astype(BF16)
        return carry

    lax.fori_loop(0, 16, key_step, 0)
    for i in range(1, 4):
        slot = lax.rem(x + i, 4)
        pair = pl.ds(pl.multiple_of(2 * slot, 2), 2)
        arrived(qg.at[pair], x_recv.at[0, slot])
        arrived(auxg.at[slot], x_recv.at[2, slot])

    document = lax.broadcasted_iota(jnp.int32, (DIM, LANES), 0)

    def span_step(s, carry):
        slot = s // 2
        seg = auxg[slot, pl.ds(2 + s % 2, 1), :].astype(jnp.int32)
        span = auxg[slot, pl.ds(4 + s % 2, 1), :]
        unseen = ((document < 4) & (document != seg)) | (local > span)
        q_aug[s, pl.ds(0, DIM), :] = qg[s].T
        q_aug[s, pl.ds(DIM, DIM), :] = jnp.where(unseen, -1e30, 0.0).astype(BF16)

        @pl.when(slot == x)
        def _():
            for c in range(0, KEYS, CHUNK):
                scores[pl.ds(c, CHUNK), :] = jnp.dot(
                    k_aug[pl.ds(c, CHUNK), :], q_aug[s], preferred_element_type=F32
                )
            rows = pl.ds(pl.multiple_of(rest * ROWS + s % 2 * SPAN, SPAN), SPAN)
            later = lax.broadcasted_iota(jnp.int32, (SPAN, LANES), 0) > (
                lax.broadcasted_iota(jnp.int32, (SPAN, LANES), 1) % SPAN
            )
            scores[rows, :] = jnp.where(later, -1e30, scores[rows, :])
            top = jnp.max(scores[...], axis=0, keepdims=True)
            weights = jnp.exp2((scores[...] - top) * (SCALE * LOG2E))
            part[0, pl.ds(s, 1), :] = top
            part[1, pl.ds(s, 1), :] = jnp.sum(weights, axis=0, keepdims=True)

        @pl.when(slot != x)
        def _():
            top = jnp.full((8, LANES), -1e30, F32)
            total = jnp.zeros((8, LANES), F32)
            for c in range(0, KEYS, BLOCK):
                block = jnp.dot(
                    k_aug[pl.ds(c, BLOCK), :], q_aug[s], preferred_element_type=F32
                ).reshape(BLOCK // 8, 8, LANES)
                new = jnp.maximum(top, jnp.max(block, axis=0))
                weights = jnp.exp2((block - new) * (SCALE * LOG2E))
                total = total * jnp.exp2((top - new) * (SCALE * LOG2E)) + jnp.sum(weights, axis=0)
                top = new
            whole_top = jnp.max(top, axis=0, keepdims=True)
            total = total * jnp.exp2((top - whole_top) * (SCALE * LOG2E))
            part[0, pl.ds(s, 1), :] = whole_top
            part[1, pl.ds(s, 1), :] = jnp.sum(total, axis=0, keepdims=True)

        return carry

    lax.fori_loop(0, 8, span_step, 0)
    got[x] = part[...]
    for i, peer in enumerate(xs):
        copies.append(send(part, got.at[x], m_send.at[i], m_recv.at[x], peer))

    for i in range(1, 16):
        slot = lax.rem(rest + i, 16)
        arrived(vg.at[slot], r_recv.at[2, slot])
    for i in range(1, 4):
        slot = lax.rem(x + i, 4)
        arrived(gg.at[pl.ds(pl.multiple_of(2 * slot, 2), 2)], x_recv.at[1, slot])
    first_three = (lax.broadcasted_iota(jnp.int32, (ROWS, DIM), 1) < 3).astype(F32).astype(BF16)

    def value_step(slot, carry):
        rows = pl.ds(pl.multiple_of(slot * ROWS, ROWS), ROWS)
        v_aug[rows, pl.ds(0, DIM)] = vg[slot]
        v_aug[rows, pl.ds(DIM, DIM)] = first_three
        return carry

    lax.fori_loop(0, 16, value_step, 0)

    def turn_keys(b, carry):
        rows = pl.ds(pl.multiple_of(b * BLOCK, BLOCK), BLOCK)
        kt[b] = k_aug[rows, pl.ds(0, DIM)].T
        return carry

    lax.fori_loop(0, KEYS // BLOCK, turn_keys, 0)

    def grad_step(s, carry):
        g_aug[s, pl.ds(0, DIM), :] = gg[s].T
        g_aug[s, pl.ds(DIM, 16), :] = pieces_of(-auxg[s // 2, pl.ds(s % 2, 1), :])
        g_aug[s, pl.ds(DIM + 16, DIM - 16), :] = jnp.zeros((DIM - 16, LANES), BF16)
        dqt[s] = jnp.zeros((DIM, LANES), F32)
        return carry

    lax.fori_loop(0, 8, grad_step, 0)
    for i in range(1, 4):
        slot = lax.rem(x + i, 4)
        arrived(got.at[slot], m_recv.at[slot])
    top = jnp.maximum(
        jnp.maximum(got[0, 0], got[1, 0]), jnp.maximum(got[2, 0], got[3, 0])
    )
    total = jnp.zeros_like(top)
    for slot in range(4):
        total = total + got[slot, 1] * jnp.exp2((got[slot, 0] - top) * (SCALE * LOG2E))
    log_total = top + jnp.log(total) * (1.0 / SCALE)
    for s in range(8):
        q_aug[s, pl.ds(DIM + LOG_ROW, 16), :] = pieces_of(-log_total[s:s + 1])

    for i, peer in enumerate(columns):
        copies.append(
            send(act_piece(act_ref, column + SHIFTS[i]), act_in.at[i + 1], act_send.at[i],
                 act_recv.at[i], peer)
        )

    def tile(pair, s, masked):
        rows = pl.ds(pl.multiple_of(pair * BLOCK, BLOCK), BLOCK)
        probs = jnp.exp2(
            jnp.dot(k_aug[rows, :], q_aug[s], preferred_element_type=F32) * (SCALE * LOG2E)
        )
        if masked:
            key = lax.broadcasted_iota(jnp.int32, (BLOCK, LANES), 0) - (
                rest % 2 * ROWS + s % 2 * SPAN
            )
            key = jnp.where(s // 2 == x, key, SPAN)
            row = lax.broadcasted_iota(jnp.int32, (BLOCK, LANES), 1) % SPAN
            probs = jnp.where((key < SPAN) & (key > row), 0.0, probs)
        prob_grad = jnp.dot(v_aug[rows, :], g_aug[s], preferred_element_type=F32)
        score_grad = (probs * prob_grad * SCALE).astype(BF16)
        dv_acc[...] += jnp.dot(probs.astype(BF16), gg[s], preferred_element_type=F32)
        dk_acc[...] += jnp.dot(score_grad, qg[s], preferred_element_type=F32)
        dqt[s] += jnp.dot(kt[pair], score_grad, preferred_element_type=F32)

    def key_block(pair):
        dk_acc[...] = jnp.zeros_like(dk_acc)
        dv_acc[...] = jnp.zeros_like(dv_acc)

        def query_step(t, carry):
            diagonal = (t == x // 2) & (pair == rest // 2)

            @pl.when(diagonal)
            def _():
                for u in range(4):
                    tile(pair, 4 * t + u, True)

            @pl.when(jnp.logical_not(diagonal))
            def _():
                for u in range(4):
                    tile(pair, 4 * t + u, False)

            return carry

        lax.fori_loop(0, 2, query_step, 0)
        for h in range(2):
            dkv_out[2 * pair + h, 0] = dk_acc[pl.ds(h * ROWS, ROWS), :].astype(BF16)
            dkv_out[2 * pair + h, 1] = dv_acc[pl.ds(h * ROWS, ROWS), :].astype(BF16)

    def to_holder(b, h):
        slot = 2 * lax.rem(rest // 2 + 1 + b, 8) + h
        return pltpu.make_async_remote_copy(
            src_ref=dkv_out.at[slot], dst_ref=dkv_in.at[rest], send_sem=d_send.at[2 * b + h],
            recv_sem=d_recv.at[rest], device_id=(x * 16 + slot, dp), device_id_type=MESH,
        )

    def block_step(b, carry):
        key_block(lax.rem(rest // 2 + 1 + b, 8))
        to_holder(b, 0).start()
        to_holder(b, 1).start()
        return carry

    lax.fori_loop(0, 7, block_step, 0)
    key_block(rest // 2)
    other = rest + 1 - 2 * (rest % 2)
    copies.append(
        send(dkv_out.at[other], dkv_in.at[rest], d_send.at[14], d_recv.at[rest],
             (x * 16 + other, dp))
    )
    dkv_in[rest] = dkv_out[rest]

    def turn_queries(s, carry):
        dq_out[s] = dqt[s].T.astype(BF16)
        return carry

    lax.fori_loop(0, 8, turn_queries, 0)
    dq_in[x] = dq_out[two]

    for i in range(1, 16):
        slot = lax.rem(rest + i, 16)
        arrived(dkv_in.at[slot], d_recv.at[slot])
    for p in range(2):
        summed = dkv_in[0, p].astype(F32)
        for slot in range(1, 16):
            summed = summed + dkv_in[slot, p].astype(F32)
        kv_low = summed.astype(BF16)
        kv_in[p, 0] = kv_low
        kvgrad_ref[:, pl.ds(p * DIM, DIM)] = kv_low
        for i, peer in enumerate(columns):
            copies.append(
                send(kv_in.at[p, 0], kv_in.at[p, i + 1], kv_send.at[p, i], kv_recv.at[p, i], peer)
            )
    for i, peer in enumerate(xs):
        there = lax.rem(x + i + 1, 4)
        copies.append(
            send(dq_out.at[pl.ds(pl.multiple_of(2 * there, 2), 2)], dq_in.at[x], dq_send.at[i],
                 dq_recv.at[x], peer)
        )

    here = z // 4 == y_hi

    def to_owner(p, i):
        there_z = lax.rem(z % 4 + i // 4, 4)
        there_dp = lax.rem(dp + i % 4, 4)
        rows = pl.ds(pl.multiple_of((there_z * 4 + there_dp) * 32, 32), 32)
        return pltpu.make_async_remote_copy(
            src_ref=partial.at[p, rows], dst_ref=g_in.at[p, line], send_sem=gr_send.at[p, i],
            recv_sem=gr_recv.at[p, line],
            device_id=(x * 16 + y_lo * 8 + y_hi * 4 + there_z, there_dp), device_id_type=MESH,
        )

    own_rows = pl.ds(pl.multiple_of((z % 4 * 4 + dp) * 32, 32), 32)
    for i in range(15):
        arrived(act_in.at[i + 1], act_recv.at[i])
    for p in range(2):
        total = jnp.zeros((DIM, LANES), F32)
        for i in range(16):
            if i > 0:
                arrived(kv_in.at[p, i], kv_recv.at[p, i - 1])
            total = total + jnp.dot(kv_in[p, i].T, act_in[i], preferred_element_type=F32)
        partial[p] = total.T.astype(BF16)
        for i in range(1, 16):
            to_owner(p, i).start()

        @pl.when(here)
        def _():
            pltpu.make_async_copy(
                partial.at[p, own_rows], g_in.at[p, line], gr_recv.at[p, line]
            ).start()

        @pl.when(jnp.logical_not(here))
        def _():
            to_owner(p, 0).start()

    sums = []
    for p in range(2):
        for slot in range(16):
            arrived(g_in.at[p, slot], gr_recv.at[p, slot])
        grad = g_in[p, 0].astype(F32)
        for slot in range(1, 16):
            grad = grad + g_in[p, slot].astype(F32)
        weight = w_ref[p]
        one = beta_one * m1_ref[p] + (1.0 - beta_one) * grad
        two = beta_two * m2_ref[p] + (1.0 - beta_two) * grad * grad
        n1_ref[p] = one
        n2_ref[p] = two
        update = one / (jnp.sqrt(two) + epsilon) + weight_decay * weight
        update_ref[p] = update
        sums.append(jnp.sum(weight * weight, axis=0, keepdims=True))
        sums.append(jnp.sum(update * update, axis=0, keepdims=True))
    a_msg[...] = jnp.concatenate(sums + [jnp.zeros((4, DIM), F32)], axis=0)
    a_in[column] = a_msg[...]
    for i, peer in enumerate(columns):
        copies.append(send(a_msg, a_in.at[column], a_send.at[i], a_recv.at[column], peer))

    for i in range(1, 4):
        slot = lax.rem(x + i, 4)
        arrived(dq_in.at[slot], dq_recv.at[slot])
    for span in range(2):
        for h in range(HEADS):
            rows = pl.ds(h * SPAN, SPAN)
            summed = dq_in[0, span, rows, :].astype(F32)
            for slot in range(1, 4):
                summed = summed + dq_in[slot, span, rows, :].astype(F32)
            qgrad_ref[pl.ds(span * SPAN, SPAN), pl.ds(h * DIM, DIM)] = summed.astype(BF16)

    for i in range(1, 16):
        slot = lax.rem(column + i, 16)
        arrived(a_in.at[slot], a_recv.at[slot])
    summed = a_in[0]
    for slot in range(1, 16):
        summed = summed + a_in[slot]
    b_msg[...] = summed
    b_in[line] = summed
    late = [
        send(b_msg, b_in.at[line], b_send.at[i], b_recv.at[line], peer)
        for i, peer in enumerate(lines)
    ]
    for copy in copies:
        copy.wait_send()
    for b in range(7):
        to_holder(b, 0).wait_send()
        to_holder(b, 1).wait_send()
    for p in range(2):
        for i in range(1, 16):
            to_owner(p, i).wait_send()

        @pl.when(jnp.logical_not(here))
        def _():
            to_owner(p, 0).wait_send()

    for i in range(1, 16):
        slot = lax.rem(line + i, 16)
        arrived(b_in.at[slot], b_recv.at[slot])
    summed = b_in[0]
    for slot in range(1, 16):
        summed = summed + b_in[slot]
    norms = jnp.sqrt(jnp.sum(summed, axis=1, keepdims=True))
    ratios = []
    for p in range(2):
        ratio = norms[2 * p:2 * p + 1] / (norms[2 * p + 1:2 * p + 2] + epsilon)
        ratios.append(ratio)
    trust_ref[...] = jnp.concatenate(
        [jnp.broadcast_to(ratio, (1, DIM)) for ratio in ratios] + [jnp.zeros((6, DIM), F32)], axis=0
    )
    for copy in late:
        copy.wait_send()


def whole(span_order, queries, out_grad, attn_out, key_states, value_states, act, segment_ids,
          kv_weight, moment_one, moment_two):
    state = jax.ShapeDtypeStruct((2, 32, DIM), F32)
    dma = pltpu.SemaphoreType.DMA
    return pl.pallas_call(
        whole_kernel,
        out_shape=(
            jax.ShapeDtypeStruct((ROWS, HEADS * DIM), BF16),
            jax.ShapeDtypeStruct((ROWS, 2 * DIM), BF16),
            state, state, state,
            jax.ShapeDtypeStruct((8, DIM), F32),
        ),
        in_specs=[smem_spec()] + [any_spec()] * 6 + [vmem_spec()] * 4,
        out_specs=(vmem_spec(),) * 6,
        scratch_shapes=[
            VMEM((ROWS, HEADS * DIM), BF16),
            VMEM((ROWS, HEADS * DIM), BF16),
            VMEM((ROWS, HEADS * DIM), BF16),
            VMEM((8, LANES, DIM), BF16),
            VMEM((8, LANES, DIM), BF16),
            VMEM((16, ROWS, DIM), BF16),
            VMEM((16, ROWS, DIM), BF16),
            VMEM((4, 8, LANES), F32),
            VMEM((16, 8, ROWS), F32),
            VMEM((KEYS, 2 * DIM), BF16),
            VMEM((KEYS, 2 * DIM), BF16),
            VMEM((8, 2 * DIM, LANES), BF16),
            VMEM((8, 2 * DIM, LANES), BF16),
            VMEM((KEYS // BLOCK, DIM, BLOCK), BF16),
            VMEM((KEYS, LANES), F32),
            VMEM((2, 8, LANES), F32),
            VMEM((4, 2, 8, LANES), F32),
            VMEM((BLOCK, DIM), F32),
            VMEM((BLOCK, DIM), F32),
            VMEM((8, DIM, LANES), F32),
            VMEM((16, 2, ROWS, DIM), BF16),
            VMEM((16, 2, ROWS, DIM), BF16),
            VMEM((8, LANES, DIM), BF16),
            VMEM((4, 2, LANES, DIM), BF16),
            VMEM((16, ROWS, LANES), BF16),
            VMEM((2, 16, ROWS, DIM), BF16),
            VMEM((2, LANES, DIM), BF16),
            VMEM((2, 16, 32, DIM), BF16),
            VMEM((16, 8, DIM), F32),
            VMEM((8, DIM), F32),
            VMEM((16, 8, DIM), F32),
            VMEM((8, DIM), F32),
            dma((3, 3)), dma((3, 4)),
            dma((3, 15)), dma((3, 16)),
            dma((15,)), dma((15,)),
            dma((3,)), dma((4,)),
            dma((15,)), dma((16,)),
            dma((3,)), dma((4,)),
            dma((2, 15)), dma((2, 15)),
            dma((2, 16)), dma((2, 16)),
            dma((15,)), dma((16,)),
            dma((15,)), dma((16,)),
            dma((6,)),
        ],
        compiler_params=pltpu.CompilerParams(
            collective_id=0, has_side_effects=True, vmem_limit_bytes=VMEM_LIMIT
        ),
        name="attention_backward",
    )(span_order, queries, out_grad, attn_out, key_states, value_states, act, segment_ids,
      kv_weight, moment_one, moment_two)


def finish_kernel(
    q_ref, kv_ref, update_ref, one_ref, two_ref, ratio_ref, weight_ref,
    qgrad_ref, kvgrad_ref, nw_ref, n1_ref, n2_ref, trust_ref,
):
    qgrad_ref[0] = q_ref[...]
    kvgrad_ref[0] = kv_ref[...]
    n1_ref[...] = one_ref[...]
    n2_ref[...] = two_ref[...]
    for p in range(2):
        ratio = ratio_ref[pl.ds(p, 1), :]
        trust_ref[p] = ratio[0, 0]
        nw_ref[p] = weight_ref[p] - learn_rate * ratio * update_ref[p]


def finish(query_grad, kv_grad, update, new_one, new_two, ratio, kv_weight):
    state = jax.ShapeDtypeStruct((2, 32, DIM), F32)
    return pl.pallas_call(
        finish_kernel,
        out_shape=(
            jax.ShapeDtypeStruct((1, ROWS, HEADS * DIM), BF16),
            jax.ShapeDtypeStruct((1, ROWS, 2 * DIM), BF16),
            state, state, state,
            jax.ShapeDtypeStruct((2,), F32),
        ),
        in_specs=[vmem_spec()] * 7,
        out_specs=(vmem_spec(),) * 5 + (smem_spec(),),
        compiler_params=pltpu.CompilerParams(vmem_limit_bytes=VMEM_LIMIT),
        name="new_weights",
    )(query_grad, kv_grad, update, new_one, new_two, ratio, kv_weight)


def on_device(
    queries,
    key_states,
    value_states,
    attn_out,
    out_grad,
    activations,
    segment_ids,
    span_order,
    kv_weight,
    moment_one,
    moment_two,
):
    query_grad, kv_grad, update, new_one, new_two, trust = whole(
        span_order, queries[0], out_grad[0], attn_out[0], key_states[0], value_states[0],
        activations[0], segment_ids, kv_weight, moment_one, moment_two,
    )
    return finish(query_grad, kv_grad, update, new_one, new_two, trust, kv_weight)


def solution(mesh):
    in_specs = (
        P("dp", "context", None),
        P("dp", "context", None),
        P("dp", "context", None),
        P("dp", "context", None),
        P("dp", "context", None),
        P("dp", "context", None),
        P("dp", "context"),
        P(),
        P(None, ("context", "dp"), None),
        P(None, ("context", "dp"), None),
        P(None, ("context", "dp"), None),
    )
    out_specs = (
        P("dp", "context", None),
        P("dp", "context", None),
        P(None, ("context", "dp"), None),
        P(None, ("context", "dp"), None),
        P(None, ("context", "dp"), None),
        P(),
    )
    return jax.shard_map(
        on_device, mesh=mesh, in_specs=in_specs, out_specs=out_specs, check_vma=False
    )
```

time: 2470 us -> 127 us (0.05)
  waiting for transfers between devices: 2020 us -> 0 us
  blocking collectives: 211 us -> 0 us
  Pallas kernels: 0 us -> 126 us
  matrix products: 115 us -> 0 us
  local copies, waits for them, and re-layouts: 72.3 us -> 0 us
  other arithmetic: 26.4 us -> 0 us
    unnamed x5 -> x0, waiting for transfers between devices: 1310 us -> none
    all_gather x2 -> x0, waiting for transfers between devices: 383 us -> none  [the longest x1 261 us: on_device(): value_piece = lax.all_gather(value_states, 'context', axis=1, tiled=True)]
    reduce_scatter x1 -> x0, waiting for transfers between devices: 328 us -> none  [on_device(): lax.psum_scatter(kv_acc, 'context', scatter_dimension=0, tiled=True)]
    all_gather x1 -> x0, blocking collectives: 133 us -> none  [on_device(): all_segments = lax.all_gather(segment_ids, 'context', axis=1, tiled=True)[0]]
    pallas_call x0 -> x2, Pallas kernels: none -> 126 us  [the longest x1 124 us: whole(): pl.pallas_call(whole_kernel, out_shape=(jax.ShapeDtypeStruct((ROWS, HEADS...]
    dot_general x97 -> x0, matrix products: 115 us -> none  [the longest x32 47 us: score_block(): jnp.einsum('qhd,kd->qhk', query_heads, key_block, preferred_element_type=...]
    psum x1 -> x0, blocking collectives: 78.2 us -> none  [on_device(): lax.psum((jnp.sum(kv_weight * kv_weight, axis=(1, 2)), jnp.sum(update * u...]
  transfers between devices with their start and end apart: 4 -> 0, of which waited for: 4 -> 0; matrix products, arithmetic and copies ran while one was open for 2% -> 0% of each run, Pallas kernels for 0% -> 0%
where the time goes in v3:
time: 127 us; the launch traced here: 126 us
  Pallas kernels  126 us (99%)
    pallas_call x1, Pallas kernels, whole(): pl.pallas_call(whole_kernel, out_shape=(jax.ShapeDtypeStruct((ROWS, HEADS...  124 us

profile of v3, /device:TPU:1, one launch (start us, length us, event | category | flops | bytes accessed | tf_op | source)
XLA Modules:
  0.0 126.4 jit_solution(1124920611017229377)
XLA Ops:
  0.6 124.0 %attention_backward.1 = (bf16[128,1024]{1,0:T(8,128)(2,1)}, bf16[128,256]{1,0:T(8,128)(2,1)}, f32[2,32,128]{2,1,0:T(8,128)}, f32[2,32,128]{2,1,0:T(8,128)}, f32[2,32,128]{2,1,0:T(8,128)}, /*index=5*/f32[8,128]{1,0:T(8,128)}) custom-call(s32[128]{0:T(128)} %order_ref.1, bf16[128,1024]{1,0:T(8,128)(2,1)} %bitcast.7, bf16[128,1024]{1,0:T(8,128)(2,1)} %bitcast.8, ...), custom_call_target="tpu_custom_call" | custom-call | tf_op jit(solution)/shard_map/attention_backward/pallas_call | solution.py:523
  124.6 1.8 %new_weights.1 = (bf16[1,128,1024]{2,1,0:T(8,128)(2,1)}, bf16[1,128,256]{2,1,0:T(8,128)(2,1)}, f32[2,32,128]{2,1,0:T(8,128)}, f32[2,32,128]{2,1,0:T(8,128)}, f32[2,32,128]{2,1,0:T(8,128)}, /*index=5*/f32[2]{0:T(128)}) custom-call(bf16[128,1024]{1,0:T(8,128)(2,1)} %get-tuple-element.12.q_ref, bf16[128,256]{1,0:T(8,128)(2,1)} %get-tuple-element.13.kv_ref, ...), custom_call_target="tpu_custom_call" | custom-call | tf_op jit(solution)/shard_map/new_weights/pallas_call | solution.py:602

commit v4 on v3

--- a/solution.py
+++ b/solution.py
@@ -21,7 +21,10 @@
 BLOCK = 256
 KEYS = 2048
 LOG_ROW = 48
-SHIFTS = (1, 15, 2, 14, 3, 13, 4, 12, 5, 11, 6, 10, 7, 9, 8)
+GROUP = 8
+FEATURES = 1024
+OWNERS = 32
+SHIFTS = (1, 7, 2, 6, 3, 5, 4)
 CHUNK = 512
 VMEM_LIMIT = 62 * 1024 * 1024
 SCALE = DIM ** (-0.5)
@@ -78,20 +81,18 @@
     return [(x * 16 + lax.rem(rest + i, 16), dp) for i in range(1, 16)]
 
 
-def column_peers(me, dp):
-    x, y_lo, z = me // 16, me // 8 % 2, me % 8
-    y_hi, core = dp // 2, dp % 2
-    column = x * 4 + y_lo * 2 + y_hi
+def member_peers(me, dp):
+    member = me // 16 * 2 + dp % 2
     peers = []
     for shift in SHIFTS:
-        there = lax.rem(column + shift, 16)
-        peers.append(((there // 4) * 16 + (there // 2 % 2) * 8 + z, (there % 2) * 2 + core))
-    return column, peers
+        there = lax.rem(member + shift, GROUP)
+        peers.append((there // 2 * 16 + me % 16, dp // 2 * 2 + there % 2))
+    return member, peers
 
 
 def act_piece(act_ref, index):
-    there = lax.rem(index, 16)
-    return act_ref.at[:, pl.ds(pl.multiple_of(there * LANES, LANES), LANES)]
+    there = lax.rem(index, GROUP)
+    return act_ref.at[:, pl.ds(pl.multiple_of(there * FEATURES, FEATURES), FEATURES)]
 
 
 def pieces_of(value):
@@ -108,7 +109,7 @@
 def whole_kernel(
     order_ref, q_ref, g_ref, o_ref, k_ref, v_ref, act_ref, seg_ref, w_ref, m1_ref, m2_ref,
     qgrad_ref, kvgrad_ref, update_ref, n1_ref, n2_ref, trust_ref,
-    q_own, g_own, o_own, qg, gg, kg, vg, auxg, segg, k_aug, v_aug, q_aug, g_aug, kt,
+    q_own, g_own, o_own, qg, gg, kg, vg, auxg, delta, segg, k_aug, v_aug, q_aug, g_aug, kt,
     scores, part, got, dk_acc, dv_acc, dqt, dkv_out, dkv_in, dq_out, dq_in,
     act_in, kv_in, partial, g_in, a_in, a_msg, b_in, b_msg,
     x_send, x_recv, r_send, r_recv, act_send, act_recv, m_send, m_recv,
@@ -118,35 +119,32 @@
     me, dp, x, rest = place()
     y_lo, z = rest // 8, rest % 8
     y_hi, core = dp // 2, dp % 2
-    line = z * 2 + core
+    line = rest * 2 + y_hi
     xs = x_peers(me, dp, x, rest)
     rs = rest_peers(me, dp, x, rest)
-    column, columns = column_peers(me, dp)
+    member, members = member_peers(me, dp)
     two = pl.ds(pl.multiple_of(2 * x, 2), 2)
 
     def in_line(index):
-        return (x * 16 + y_lo * 8 + index // 2, y_hi * 2 + index % 2)
-
-    lines = [in_line(lax.rem(line + i, 16)) for i in range(1, 16)]
+        return (x * 16 + index // 2, index % 2 * 2 + core)
+
+    lines = [in_line(lax.rem(line + i, OWNERS)) for i in range(1, OWNERS)]
     own = [
+        pltpu.make_async_copy(q_ref, q_own, own_sem.at[2]),
         pltpu.make_async_copy(k_ref, kg.at[rest], own_sem.at[0]),
-        pltpu.make_async_copy(q_ref, q_own, own_sem.at[2]),
         pltpu.make_async_copy(g_ref, g_own, own_sem.at[3]),
         pltpu.make_async_copy(o_ref, o_own, own_sem.at[4]),
         pltpu.make_async_copy(v_ref, vg.at[rest], own_sem.at[5]),
-        pltpu.make_async_copy(act_piece(act_ref, column), act_in.at[0], own_sem.at[1]),
+        pltpu.make_async_copy(act_piece(act_ref, member), act_in.at[0], own_sem.at[1]),
     ]
     for copy in own:
         copy.start()
     greeted = [
-        (x * 16 + y_lo * 8 + lax.rem(z + i // 4, 8), lax.rem(dp + i % 4, 4)) for i in range(1, 32)
+        (x * 16 + lax.rem(rest + i // 4, 16), lax.rem(dp + i % 4, 4)) for i in range(1, 64)
     ]
-    greeted += [(x * 16 + (1 - y_lo) * 8 + i, dp) for i in range(8)]
     greeted += [
-        (lax.rem(x + i, 4) * 16 + j * 8 + z, k * 2 + core)
-        for i in range(1, 4) for j in range(2) for k in range(2)
+        (lax.rem(x + i, 4) * 16 + rest, y_hi * 2 + j) for i in range(1, 4) for j in range(2)
     ]
-    greeted += [(x * 16 + (1 - y_lo) * 8 + z, (1 - y_hi) * 2 + core)]
     barrier = greet(greeted)
     seg_own = jnp.broadcast_to(seg_ref[...], (8, ROWS)).astype(F32)
     segg[rest] = seg_own
@@ -154,30 +152,19 @@
     lower = lax.broadcasted_iota(jnp.int32, (8, ROWS), 1) < SPAN
     row_of = lax.broadcasted_iota(jnp.int32, (8, LANES), 0)
     auxg[x] = jnp.where(
-        row_of == 2, jnp.concatenate([jnp.where(lower, seg_own, swapped)] * 4, axis=1),
+        row_of == 0, jnp.concatenate([jnp.where(lower, seg_own, swapped)] * 4, axis=1),
         jnp.where(
-            row_of == 3, jnp.concatenate([jnp.where(lower, swapped, seg_own)] * 4, axis=1),
-            jnp.where(row_of == 4, order_ref[2 * me], order_ref[2 * me + 1]).astype(F32),
+            row_of == 1, jnp.concatenate([jnp.where(lower, swapped, seg_own)] * 4, axis=1),
+            jnp.where(row_of == 2, order_ref[2 * me], order_ref[2 * me + 1]).astype(F32),
         ),
     )
-    span_row = lax.broadcasted_iota(jnp.int32, (DIM, DIM), 0)
-    local = jnp.full((DIM, DIM), -1, jnp.int32)
-    for t in range(32):
-        local = jnp.where(span_row == t + 4, order_ref[32 * x + t], local)
-    local = jnp.concatenate([local] * (LANES // DIM), axis=1).astype(F32)
-    for copy in own:
-        copy.wait()
+    own[0].wait()
+    own[1].wait()
     for span in range(2):
-        rows = pl.ds(span * SPAN, SPAN)
-        products = []
         for h in range(HEADS):
-            cols = pl.ds(h * DIM, DIM)
-            qg[2 * x + span, pl.ds(h * SPAN, SPAN), :] = q_own[rows, cols]
-            grad = g_own[rows, cols]
-            gg[2 * x + span, pl.ds(h * SPAN, SPAN), :] = grad
-            products.append(grad.astype(F32) * o_own[rows, cols].astype(F32))
-        product = jnp.concatenate(products, axis=0)
-        auxg[x, pl.ds(span, 1), :] = jnp.sum(product.T, axis=0, keepdims=True)
+            qg[2 * x + span, pl.ds(h * SPAN, SPAN), :] = q_own[
+                pl.ds(span * SPAN, SPAN), pl.ds(h * DIM, DIM)
+            ]
     pl.semaphore_wait(barrier, len(greeted))
 
     copies = []
@@ -187,10 +174,34 @@
             copies.append(send(auxg.at[x], auxg.at[x], x_send.at[2, i], x_recv.at[2, x], xs[i]))
         copies.append(send(kg.at[rest], kg.at[rest], r_send.at[0, i], r_recv.at[0, rest], peer))
         copies.append(send(segg.at[rest], segg.at[rest], r_send.at[1, i], r_recv.at[1, rest], peer))
+    for copy in own[2:]:
+        copy.wait()
+    for span in range(2):
+        for h in range(HEADS):
+            gg[2 * x + span, pl.ds(h * SPAN, SPAN), :] = g_own[
+                pl.ds(span * SPAN, SPAN), pl.ds(h * DIM, DIM)
+            ]
     for i, peer in enumerate(rs):
         if i < 3:
             copies.append(send(gg.at[two], gg.at[two], x_send.at[1, i], x_recv.at[1, x], xs[i]))
         copies.append(send(vg.at[rest], vg.at[rest], r_send.at[2, i], r_recv.at[2, rest], peer))
+    delta[x] = jnp.zeros((8, LANES), F32)
+    for span in range(2):
+        rows = pl.ds(span * SPAN, SPAN)
+        products = []
+        for h in range(HEADS):
+            cols = pl.ds(h * DIM, DIM)
+            products.append(g_own[rows, cols].astype(F32) * o_own[rows, cols].astype(F32))
+        product = jnp.concatenate(products, axis=0)
+        delta[x, pl.ds(span, 1), :] = jnp.sum(product.T, axis=0, keepdims=True)
+    for i, peer in enumerate(xs):
+        copies.append(send(delta.at[x], delta.at[x], x_send.at[3, i], x_recv.at[3, x], peer))
+    span_row = lax.broadcasted_iota(jnp.int32, (DIM, DIM), 0)
+    local = jnp.full((DIM, DIM), -1, jnp.int32)
+    for t in range(32):
+        local = jnp.where(span_row == t + 4, order_ref[32 * x + t], local)
+    local = jnp.concatenate([local] * (LANES // DIM), axis=1).astype(F32)
+
     for i in range(1, 16):
         slot = lax.rem(rest + i, 16)
         arrived(kg.at[slot], r_recv.at[0, slot])
@@ -218,8 +229,8 @@
 
     def span_step(s, carry):
         slot = s // 2
-        seg = auxg[slot, pl.ds(2 + s % 2, 1), :].astype(jnp.int32)
-        span = auxg[slot, pl.ds(4 + s % 2, 1), :]
+        seg = auxg[slot, pl.ds(s % 2, 1), :].astype(jnp.int32)
+        span = auxg[slot, pl.ds(2 + s % 2, 1), :]
         unseen = ((document < 4) & (document != seg)) | (local > span)
         q_aug[s, pl.ds(0, DIM), :] = qg[s].T
         q_aug[s, pl.ds(DIM, DIM), :] = jnp.where(unseen, -1e30, 0.0).astype(BF16)
@@ -270,6 +281,7 @@
     for i in range(1, 4):
         slot = lax.rem(x + i, 4)
         arrived(gg.at[pl.ds(pl.multiple_of(2 * slot, 2), 2)], x_recv.at[1, slot])
+        arrived(delta.at[slot], x_recv.at[3, slot])
     first_three = (lax.broadcasted_iota(jnp.int32, (ROWS, DIM), 1) < 3).astype(F32).astype(BF16)
 
     def value_step(slot, carry):
@@ -289,7 +301,7 @@
 
     def grad_step(s, carry):
         g_aug[s, pl.ds(0, DIM), :] = gg[s].T
-        g_aug[s, pl.ds(DIM, 16), :] = pieces_of(-auxg[s // 2, pl.ds(s % 2, 1), :])
+        g_aug[s, pl.ds(DIM, 16), :] = pieces_of(-delta[s // 2, pl.ds(s % 2, 1), :])
         g_aug[s, pl.ds(DIM + 16, DIM - 16), :] = jnp.zeros((DIM - 16, LANES), BF16)
         dqt[s] = jnp.zeros((DIM, LANES), F32)
         return carry
@@ -308,9 +320,9 @@
     for s in range(8):
         q_aug[s, pl.ds(DIM + LOG_ROW, 16), :] = pieces_of(-log_total[s:s + 1])
 
-    for i, peer in enumerate(columns):
+    for i, peer in enumerate(members):
         copies.append(
-            send(act_piece(act_ref, column + SHIFTS[i]), act_in.at[i + 1], act_send.at[i],
+            send(act_piece(act_ref, member + SHIFTS[i]), act_in.at[i + 1], act_send.at[i],
                  act_recv.at[i], peer)
         )
 
@@ -395,7 +407,7 @@
         kv_low = summed.astype(BF16)
         kv_in[p, 0] = kv_low
         kvgrad_ref[:, pl.ds(p * DIM, DIM)] = kv_low
-        for i, peer in enumerate(columns):
+        for i, peer in enumerate(members):
             copies.append(
                 send(kv_in.at[p, 0], kv_in.at[p, i + 1], kv_send.at[p, i], kv_recv.at[p, i], peer)
             )
@@ -406,29 +418,29 @@
                  dq_recv.at[x], peer)
         )
 
-    here = z // 4 == y_hi
+    here = y_lo == core
 
     def to_owner(p, i):
-        there_z = lax.rem(z % 4 + i // 4, 4)
+        there_z = lax.rem(z + i // 4, 8)
         there_dp = lax.rem(dp + i % 4, 4)
         rows = pl.ds(pl.multiple_of((there_z * 4 + there_dp) * 32, 32), 32)
         return pltpu.make_async_remote_copy(
             src_ref=partial.at[p, rows], dst_ref=g_in.at[p, line], send_sem=gr_send.at[p, i],
             recv_sem=gr_recv.at[p, line],
-            device_id=(x * 16 + y_lo * 8 + y_hi * 4 + there_z, there_dp), device_id_type=MESH,
+            device_id=(x * 16 + core * 8 + there_z, there_dp), device_id_type=MESH,
         )
 
-    own_rows = pl.ds(pl.multiple_of((z % 4 * 4 + dp) * 32, 32), 32)
-    for i in range(15):
+    own_rows = pl.ds(pl.multiple_of((z * 4 + dp) * 32, 32), 32)
+    for i in range(GROUP - 1):
         arrived(act_in.at[i + 1], act_recv.at[i])
     for p in range(2):
-        total = jnp.zeros((DIM, LANES), F32)
-        for i in range(16):
+        total = jnp.zeros((DIM, FEATURES), F32)
+        for i in range(GROUP):
             if i > 0:
                 arrived(kv_in.at[p, i], kv_recv.at[p, i - 1])
             total = total + jnp.dot(kv_in[p, i].T, act_in[i], preferred_element_type=F32)
         partial[p] = total.T.astype(BF16)
-        for i in range(1, 16):
+        for i in range(1, OWNERS):
             to_owner(p, i).start()
 
         @pl.when(here)
@@ -443,10 +455,10 @@
 
     sums = []
     for p in range(2):
-        for slot in range(16):
+        for slot in range(OWNERS):
             arrived(g_in.at[p, slot], gr_recv.at[p, slot])
         grad = g_in[p, 0].astype(F32)
-        for slot in range(1, 16):
+        for slot in range(1, OWNERS):
             grad = grad + g_in[p, slot].astype(F32)
         weight = w_ref[p]
         one = beta_one * m1_ref[p] + (1.0 - beta_one) * grad
@@ -458,10 +470,22 @@
         sums.append(jnp.sum(weight * weight, axis=0, keepdims=True))
         sums.append(jnp.sum(update * update, axis=0, keepdims=True))
     a_msg[...] = jnp.concatenate(sums + [jnp.zeros((4, DIM), F32)], axis=0)
-    a_in[column] = a_msg[...]
-    for i, peer in enumerate(columns):
-        copies.append(send(a_msg, a_in.at[column], a_send.at[i], a_recv.at[column], peer))
-
+    a_in[member] = a_msg[...]
+    for i, peer in enumerate(members):
+        copies.append(send(a_msg, a_in.at[member], a_send.at[i], a_recv.at[member], peer))
+
+    for i in range(1, GROUP):
+        slot = lax.rem(member + i, GROUP)
+        arrived(a_in.at[slot], a_recv.at[slot])
+    summed = a_in[0]
+    for slot in range(1, GROUP):
+        summed = summed + a_in[slot]
+    b_msg[...] = summed
+    b_in[line] = summed
+    late = [
+        send(b_msg, b_in.at[line], b_send.at[i], b_recv.at[line], peer)
+        for i, peer in enumerate(lines)
+    ]
     for i in range(1, 4):
         slot = lax.rem(x + i, 4)
         arrived(dq_in.at[slot], dq_recv.at[slot])
@@ -473,36 +497,24 @@
                 summed = summed + dq_in[slot, span, rows, :].astype(F32)
             qgrad_ref[pl.ds(span * SPAN, SPAN), pl.ds(h * DIM, DIM)] = summed.astype(BF16)
 
-    for i in range(1, 16):
-        slot = lax.rem(column + i, 16)
-        arrived(a_in.at[slot], a_recv.at[slot])
-    summed = a_in[0]
-    for slot in range(1, 16):
-        summed = summed + a_in[slot]
-    b_msg[...] = summed
-    b_in[line] = summed
-    late = [
-        send(b_msg, b_in.at[line], b_send.at[i], b_recv.at[line], peer)
-        for i, peer in enumerate(lines)
-    ]
     for copy in copies:
         copy.wait_send()
     for b in range(7):
         to_holder(b, 0).wait_send()
         to_holder(b, 1).wait_send()
     for p in range(2):
-        for i in range(1, 16):
+        for i in range(1, OWNERS):
             to_owner(p, i).wait_send()
 
         @pl.when(jnp.logical_not(here))
         def _():
             to_owner(p, 0).wait_send()
 
-    for i in range(1, 16):
-        slot = lax.rem(line + i, 16)
+    for i in range(1, OWNERS):
+        slot = lax.rem(line + i, OWNERS)
         arrived(b_in.at[slot], b_recv.at[slot])
     summed = b_in[0]
-    for slot in range(1, 16):
+    for slot in range(1, OWNERS):
         summed = summed + b_in[slot]
     norms = jnp.sqrt(jnp.sum(summed, axis=1, keepdims=True))
     ratios = []
@@ -539,6 +551,7 @@
             VMEM((16, ROWS, DIM), BF16),
             VMEM((16, ROWS, DIM), BF16),
             VMEM((4, 8, LANES), F32),
+            VMEM((4, 8, LANES), F32),
             VMEM((16, 8, ROWS), F32),
             VMEM((KEYS, 2 * DIM), BF16),
             VMEM((KEYS, 2 * DIM), BF16),
@@ -555,24 +568,24 @@
             VMEM((16, 2, ROWS, DIM), BF16),
             VMEM((8, LANES, DIM), BF16),
             VMEM((4, 2, LANES, DIM), BF16),
-            VMEM((16, ROWS, LANES), BF16),
-            VMEM((2, 16, ROWS, DIM), BF16),
-            VMEM((2, LANES, DIM), BF16),
-            VMEM((2, 16, 32, DIM), BF16),
-            VMEM((16, 8, DIM), F32),
+            VMEM((GROUP, ROWS, FEATURES), BF16),
+            VMEM((2, GROUP, ROWS, DIM), BF16),
+            VMEM((2, FEATURES, DIM), BF16),
+            VMEM((2, OWNERS, 32, DIM), BF16),
+            VMEM((GROUP, 8, DIM), F32),
             VMEM((8, DIM), F32),
-            VMEM((16, 8, DIM), F32),
+            VMEM((OWNERS, 8, DIM), F32),
             VMEM((8, DIM), F32),
-            dma((3, 3)), dma((3, 4)),
+            dma((4, 3)), dma((4, 4)),
             dma((3, 15)), dma((3, 16)),
-            dma((15,)), dma((15,)),
+            dma((7,)), dma((7,)),
             dma((3,)), dma((4,)),
             dma((15,)), dma((16,)),
             dma((3,)), dma((4,)),
-            dma((2, 15)), dma((2, 15)),
-            dma((2, 16)), dma((2, 16)),
-            dma((15,)), dma((16,)),
-            dma((15,)), dma((16,)),
+            dma((2, 7)), dma((2, 7)),
+            dma((2, OWNERS)), dma((2, OWNERS)),
+            dma((7,)), dma((GROUP,)),
+            dma((31,)), dma((OWNERS,)),
             dma((6,)),
         ],
         compiler_params=pltpu.CompilerParams(

time: 127 us -> 118 us (0.929)
  Pallas kernels: 126 us -> 117 us
    pallas_call x1, Pallas kernels: 124 us -> 115 us  [whole(): pl.pallas_call(whole_kernel, out_shape=(jax.ShapeDtypeStruct((ROWS, HEADS...]
where the time goes in v4:
time: 118 us; the launch traced here: 117 us
  Pallas kernels  117 us (99%)
    pallas_call x1, Pallas kernels, whole(): pl.pallas_call(whole_kernel, out_shape=(jax.ShapeDtypeStruct((ROWS, HEADS...  115 us

profile of v4, /device:TPU:1, one launch (start us, length us, event | category | flops | bytes accessed | tf_op | source)
XLA Modules:
  0.0 117.5 jit_solution(2783289532020253443)
XLA Ops:
  0.6 114.9 %attention_backward.1 = (bf16[128,1024]{1,0:T(8,128)(2,1)}, bf16[128,256]{1,0:T(8,128)(2,1)}, f32[2,32,128]{2,1,0:T(8,128)}, f32[2,32,128]{2,1,0:T(8,128)}, f32[2,32,128]{2,1,0:T(8,128)}, /*index=5*/f32[8,128]{1,0:T(8,128)}) custom-call(s32[128]{0:T(128)} %order_ref.1, bf16[128,1024]{1,0:T(8,128)(2,1)} %bitcast.7, bf16[128,1024]{1,0:T(8,128)(2,1)} %bitcast.8, ...), custom_call_target="tpu_custom_call" | custom-call | tf_op jit(solution)/shard_map/attention_backward/pallas_call | solution.py:535
  115.5 1.8 %new_weights.1 = (bf16[1,128,1024]{2,1,0:T(8,128)(2,1)}, bf16[1,128,256]{2,1,0:T(8,128)(2,1)}, f32[2,32,128]{2,1,0:T(8,128)}, f32[2,32,128]{2,1,0:T(8,128)}, f32[2,32,128]{2,1,0:T(8,128)}, /*index=5*/f32[2]{0:T(128)}) custom-call(bf16[128,1024]{1,0:T(8,128)(2,1)} %get-tuple-element.12.q_ref, bf16[128,256]{1,0:T(8,128)(2,1)} %get-tuple-element.13.kv_ref, ...), custom_call_target="tpu_custom_call" | custom-call | tf_op jit(solution)/shard_map/new_weights/pallas_call | solution.py:615

commit v5 on v4

--- a/solution.py
+++ b/solution.py
@@ -24,6 +24,9 @@
 GROUP = 8
 FEATURES = 1024
 OWNERS = 32
+FAR_FIRST = sorted(
+    range(1, OWNERS), key=lambda i: -min(i // 2 % 8, 8 - i // 2 % 8) - (0, 2, 1, 1)[i // 16 * 2 + i % 2]
+)
 SHIFTS = (1, 7, 2, 6, 3, 5, 4)
 CHUNK = 512
 VMEM_LIMIT = 62 * 1024 * 1024
@@ -107,9 +110,9 @@
 
 
 def whole_kernel(
-    order_ref, q_ref, g_ref, o_ref, k_ref, v_ref, act_ref, seg_ref, w_ref, m1_ref, m2_ref,
+    order_ref, q_ref, g_ref, o_ref, k_ref, v_ref, act_ref, seg_ref, w_hbm, m1_hbm, m2_hbm,
     qgrad_ref, kvgrad_ref, update_ref, n1_ref, n2_ref, trust_ref,
-    q_own, g_own, o_own, qg, gg, kg, vg, auxg, delta, segg, k_aug, v_aug, q_aug, g_aug, kt,
+    w_ref, m1_ref, m2_ref, q_own, g_own, o_own, qg, gg, kg, vg, auxg, delta, segg, k_aug, v_aug, q_aug, g_aug, kt,
     scores, part, got, dk_acc, dv_acc, dqt, dkv_out, dkv_in, dq_out, dq_in,
     act_in, kv_in, partial, g_in, a_in, a_msg, b_in, b_msg,
     x_send, x_recv, r_send, r_recv, act_send, act_recv, m_send, m_recv,
@@ -128,7 +131,7 @@
     def in_line(index):
         return (x * 16 + index // 2, index % 2 * 2 + core)
 
-    lines = [in_line(lax.rem(line + i, OWNERS)) for i in range(1, OWNERS)]
+    lines = [in_line(lax.rem(line + i, OWNERS)) for i in FAR_FIRST]
     own = [
         pltpu.make_async_copy(q_ref, q_own, own_sem.at[2]),
         pltpu.make_async_copy(k_ref, kg.at[rest], own_sem.at[0]),
@@ -136,6 +139,9 @@
         pltpu.make_async_copy(o_ref, o_own, own_sem.at[4]),
         pltpu.make_async_copy(v_ref, vg.at[rest], own_sem.at[5]),
         pltpu.make_async_copy(act_piece(act_ref, member), act_in.at[0], own_sem.at[1]),
+        pltpu.make_async_copy(w_hbm, w_ref, own_sem.at[6]),
+        pltpu.make_async_copy(m1_hbm, m1_ref, own_sem.at[7]),
+        pltpu.make_async_copy(m2_hbm, m2_ref, own_sem.at[8]),
     ]
     for copy in own:
         copy.start()
@@ -202,10 +208,6 @@
         local = jnp.where(span_row == t + 4, order_ref[32 * x + t], local)
     local = jnp.concatenate([local] * (LANES // DIM), axis=1).astype(F32)
 
-    for i in range(1, 16):
-        slot = lax.rem(rest + i, 16)
-        arrived(kg.at[slot], r_recv.at[0, slot])
-        arrived(segg.at[slot], r_recv.at[1, slot])
     feature = lax.broadcasted_iota(jnp.int32, (DIM, ROWS), 0)
     half = lax.broadcasted_iota(jnp.int32, (DIM, ROWS), 1) // SPAN
     ones = (feature >= LOG_ROW) & (feature < LOG_ROW + 3)
@@ -218,16 +220,19 @@
         k_aug[rows, pl.ds(DIM, DIM)] = hot.astype(F32).T.astype(BF16)
         return carry
 
-    lax.fori_loop(0, 16, key_step, 0)
-    for i in range(1, 4):
-        slot = lax.rem(x + i, 4)
-        pair = pl.ds(pl.multiple_of(2 * slot, 2), 2)
-        arrived(qg.at[pair], x_recv.at[0, slot])
-        arrived(auxg.at[slot], x_recv.at[2, slot])
+    key_step(rest, 0)
+
+    def arriving_step(i, carry):
+        slot = lax.rem(rest + i, 16)
+        arrived(kg.at[slot], r_recv.at[0, slot])
+        arrived(segg.at[slot], r_recv.at[1, slot])
+        return key_step(slot, carry)
+
+    lax.fori_loop(1, 16, arriving_step, 0)
 
     document = lax.broadcasted_iota(jnp.int32, (DIM, LANES), 0)
 
-    def span_step(s, carry):
+    def query_features(s):
         slot = s // 2
         seg = auxg[slot, pl.ds(s % 2, 1), :].astype(jnp.int32)
         span = auxg[slot, pl.ds(2 + s % 2, 1), :]
@@ -235,62 +240,56 @@
         q_aug[s, pl.ds(0, DIM), :] = qg[s].T
         q_aug[s, pl.ds(DIM, DIM), :] = jnp.where(unseen, -1e30, 0.0).astype(BF16)
 
-        @pl.when(slot == x)
-        def _():
-            for c in range(0, KEYS, CHUNK):
-                scores[pl.ds(c, CHUNK), :] = jnp.dot(
-                    k_aug[pl.ds(c, CHUNK), :], q_aug[s], preferred_element_type=F32
-                )
-            rows = pl.ds(pl.multiple_of(rest * ROWS + s % 2 * SPAN, SPAN), SPAN)
-            later = lax.broadcasted_iota(jnp.int32, (SPAN, LANES), 0) > (
-                lax.broadcasted_iota(jnp.int32, (SPAN, LANES), 1) % SPAN
+    def own_step(h, carry):
+        s = 2 * x + h
+        query_features(s)
+        for c in range(0, KEYS, CHUNK):
+            scores[pl.ds(c, CHUNK), :] = jnp.dot(
+                k_aug[pl.ds(c, CHUNK), :], q_aug[s], preferred_element_type=F32
             )
-            scores[rows, :] = jnp.where(later, -1e30, scores[rows, :])
-            top = jnp.max(scores[...], axis=0, keepdims=True)
-            weights = jnp.exp2((scores[...] - top) * (SCALE * LOG2E))
-            part[0, pl.ds(s, 1), :] = top
-            part[1, pl.ds(s, 1), :] = jnp.sum(weights, axis=0, keepdims=True)
-
-        @pl.when(slot != x)
-        def _():
-            top = jnp.full((8, LANES), -1e30, F32)
-            total = jnp.zeros((8, LANES), F32)
-            for c in range(0, KEYS, BLOCK):
-                block = jnp.dot(
-                    k_aug[pl.ds(c, BLOCK), :], q_aug[s], preferred_element_type=F32
-                ).reshape(BLOCK // 8, 8, LANES)
-                new = jnp.maximum(top, jnp.max(block, axis=0))
-                weights = jnp.exp2((block - new) * (SCALE * LOG2E))
-                total = total * jnp.exp2((top - new) * (SCALE * LOG2E)) + jnp.sum(weights, axis=0)
-                top = new
-            whole_top = jnp.max(top, axis=0, keepdims=True)
-            total = total * jnp.exp2((top - whole_top) * (SCALE * LOG2E))
-            part[0, pl.ds(s, 1), :] = whole_top
-            part[1, pl.ds(s, 1), :] = jnp.sum(total, axis=0, keepdims=True)
-
+        rows = pl.ds(pl.multiple_of(rest * ROWS + h * SPAN, SPAN), SPAN)
+        later = lax.broadcasted_iota(jnp.int32, (SPAN, LANES), 0) > (
+            lax.broadcasted_iota(jnp.int32, (SPAN, LANES), 1) % SPAN
+        )
+        scores[rows, :] = jnp.where(later, -1e30, scores[rows, :])
+        top = jnp.max(scores[...], axis=0, keepdims=True)
+        weights = jnp.exp2((scores[...] - top) * (SCALE * LOG2E))
+        part[0, pl.ds(s, 1), :] = top
+        part[1, pl.ds(s, 1), :] = jnp.sum(weights, axis=0, keepdims=True)
         return carry
 
-    lax.fori_loop(0, 8, span_step, 0)
+    lax.fori_loop(0, 2, own_step, 0)
+
+    def span_step(s, carry):
+        query_features(s)
+        top = jnp.full((8, LANES), -1e30, F32)
+        total = jnp.zeros((8, LANES), F32)
+        for c in range(0, KEYS, BLOCK):
+            block = jnp.dot(
+                k_aug[pl.ds(c, BLOCK), :], q_aug[s], preferred_element_type=F32
+            ).reshape(BLOCK // 8, 8, LANES)
+            new = jnp.maximum(top, jnp.max(block, axis=0))
+            weights = jnp.exp2((block - new) * (SCALE * LOG2E))
+            total = total * jnp.exp2((top - new) * (SCALE * LOG2E)) + jnp.sum(weights, axis=0)
+            top = new
+        whole_top = jnp.max(top, axis=0, keepdims=True)
+        total = total * jnp.exp2((top - whole_top) * (SCALE * LOG2E))
+        part[0, pl.ds(s, 1), :] = whole_top
+        part[1, pl.ds(s, 1), :] = jnp.sum(total, axis=0, keepdims=True)
+        return carry
+
+    def rows_step(i, carry):
+        slot = lax.rem(x + i, 4)
+        pair = pl.ds(pl.multiple_of(2 * slot, 2), 2)
+        arrived(qg.at[pair], x_recv.at[0, slot])
+        arrived(auxg.at[slot], x_recv.at[2, slot])
+        return lax.fori_loop(2 * slot, 2 * slot + 2, span_step, carry)
+
+    lax.fori_loop(1, 4, rows_step, 0)
+    early, copies = copies, []
     got[x] = part[...]
     for i, peer in enumerate(xs):
         copies.append(send(part, got.at[x], m_send.at[i], m_recv.at[x], peer))
-
-    for i in range(1, 16):
-        slot = lax.rem(rest + i, 16)
-        arrived(vg.at[slot], r_recv.at[2, slot])
-    for i in range(1, 4):
-        slot = lax.rem(x + i, 4)
-        arrived(gg.at[pl.ds(pl.multiple_of(2 * slot, 2), 2)], x_recv.at[1, slot])
-        arrived(delta.at[slot], x_recv.at[3, slot])
-    first_three = (lax.broadcasted_iota(jnp.int32, (ROWS, DIM), 1) < 3).astype(F32).astype(BF16)
-
-    def value_step(slot, carry):
-        rows = pl.ds(pl.multiple_of(slot * ROWS, ROWS), ROWS)
-        v_aug[rows, pl.ds(0, DIM)] = vg[slot]
-        v_aug[rows, pl.ds(DIM, DIM)] = first_three
-        return carry
-
-    lax.fori_loop(0, 16, value_step, 0)
 
     def turn_keys(b, carry):
         rows = pl.ds(pl.multiple_of(b * BLOCK, BLOCK), BLOCK)
@@ -298,15 +297,40 @@
         return carry
 
     lax.fori_loop(0, KEYS // BLOCK, turn_keys, 0)
-
-    def grad_step(s, carry):
+    first_three = (lax.broadcasted_iota(jnp.int32, (ROWS, DIM), 1) < 3).astype(F32).astype(BF16)
+
+    def value_step(slot):
+        rows = pl.ds(pl.multiple_of(slot * ROWS, ROWS), ROWS)
+        v_aug[rows, pl.ds(0, DIM)] = vg[slot]
+        v_aug[rows, pl.ds(DIM, DIM)] = first_three
+
+    def grad_step(s):
         g_aug[s, pl.ds(0, DIM), :] = gg[s].T
         g_aug[s, pl.ds(DIM, 16), :] = pieces_of(-delta[s // 2, pl.ds(s % 2, 1), :])
         g_aug[s, pl.ds(DIM + 16, DIM - 16), :] = jnp.zeros((DIM - 16, LANES), BF16)
         dqt[s] = jnp.zeros((DIM, LANES), F32)
+
+    value_step(rest)
+    grad_step(2 * x)
+    grad_step(2 * x + 1)
+
+    def arriving_values(i, carry):
+        slot = lax.rem(rest + i, 16)
+        arrived(vg.at[slot], r_recv.at[2, slot])
+        value_step(slot)
         return carry
 
-    lax.fori_loop(0, 8, grad_step, 0)
+    lax.fori_loop(1, 16, arriving_values, 0)
+
+    def arriving_grads(i, carry):
+        slot = lax.rem(x + i, 4)
+        arrived(gg.at[pl.ds(pl.multiple_of(2 * slot, 2), 2)], x_recv.at[1, slot])
+        arrived(delta.at[slot], x_recv.at[3, slot])
+        grad_step(2 * slot)
+        grad_step(2 * slot + 1)
+        return carry
+
+    lax.fori_loop(1, 4, arriving_grads, 0)
     for i in range(1, 4):
         slot = lax.rem(x + i, 4)
         arrived(got.at[slot], m_recv.at[slot])
@@ -368,15 +392,20 @@
             dkv_out[2 * pair + h, 0] = dk_acc[pl.ds(h * ROWS, ROWS), :].astype(BF16)
             dkv_out[2 * pair + h, 1] = dv_acc[pl.ds(h * ROWS, ROWS), :].astype(BF16)
 
+    def block_of(b):
+        turn = b // 2
+        offset = (2 + turn + 5 * (turn // 2) + 2 * (turn // 3)) % 4 + 4 * ((b + b // 6) % 2)
+        return lax.rem(rest // 2 + offset, 8)
+
     def to_holder(b, h):
-        slot = 2 * lax.rem(rest // 2 + 1 + b, 8) + h
+        slot = 2 * block_of(b) + h
         return pltpu.make_async_remote_copy(
             src_ref=dkv_out.at[slot], dst_ref=dkv_in.at[rest], send_sem=d_send.at[2 * b + h],
             recv_sem=d_recv.at[rest], device_id=(x * 16 + slot, dp), device_id_type=MESH,
         )
 
     def block_step(b, carry):
-        key_block(lax.rem(rest // 2 + 1 + b, 8))
+        key_block(block_of(b))
         to_holder(b, 0).start()
         to_holder(b, 1).start()
         return carry
@@ -389,6 +418,9 @@
              (x * 16 + other, dp))
     )
     dkv_in[rest] = dkv_out[rest]
+
+    for copy in early:
+        copy.wait_send()
 
     def turn_queries(s, carry):
         dq_out[s] = dqt[s].T.astype(BF16)
@@ -453,6 +485,24 @@
         def _():
             to_owner(p, 0).start()
 
+    for copy in copies:
+        copy.wait_send()
+    copies = []
+    for b in range(7):
+        to_holder(b, 0).wait_send()
+        to_holder(b, 1).wait_send()
+
+    for i in range(1, 4):
+        slot = lax.rem(x + i, 4)
+        arrived(dq_in.at[slot], dq_recv.at[slot])
+    for span in range(2):
+        for h in range(HEADS):
+            rows = pl.ds(h * SPAN, SPAN)
+            summed = dq_in[0, span, rows, :].astype(F32)
+            for slot in range(1, 4):
+                summed = summed + dq_in[slot, span, rows, :].astype(F32)
+            qgrad_ref[pl.ds(span * SPAN, SPAN), pl.ds(h * DIM, DIM)] = summed.astype(BF16)
+
     sums = []
     for p in range(2):
         for slot in range(OWNERS):
@@ -486,22 +536,8 @@
         send(b_msg, b_in.at[line], b_send.at[i], b_recv.at[line], peer)
         for i, peer in enumerate(lines)
     ]
-    for i in range(1, 4):
-        slot = lax.rem(x + i, 4)
-        arrived(dq_in.at[slot], dq_recv.at[slot])
-    for span in range(2):
-        for h in range(HEADS):
-            rows = pl.ds(h * SPAN, SPAN)
-            summed = dq_in[0, span, rows, :].astype(F32)
-            for slot in range(1, 4):
-                summed = summed + dq_in[slot, span, rows, :].astype(F32)
-            qgrad_ref[pl.ds(span * SPAN, SPAN), pl.ds(h * DIM, DIM)] = summed.astype(BF16)
-
     for copy in copies:
         copy.wait_send()
-    for b in range(7):
-        to_holder(b, 0).wait_send()
-        to_holder(b, 1).wait_send()
     for p in range(2):
         for i in range(1, OWNERS):
             to_owner(p, i).wait_send()
@@ -540,9 +576,12 @@
             state, state, state,
             jax.ShapeDtypeStruct((8, DIM), F32),
         ),
-        in_specs=[smem_spec()] + [any_spec()] * 6 + [vmem_spec()] * 4,
+        in_specs=[smem_spec()] + [any_spec()] * 6 + [vmem_spec()] + [any_spec()] * 3,
         out_specs=(vmem_spec(),) * 6,
         scratch_shapes=[
+            VMEM((2, 32, DIM), F32),
+            VMEM((2, 32, DIM), F32),
+            VMEM((2, 32, DIM), F32),
             VMEM((ROWS, HEADS * DIM), BF16),
             VMEM((ROWS, HEADS * DIM), BF16),
             VMEM((ROWS, HEADS * DIM), BF16),
@@ -586,7 +625,7 @@
             dma((2, OWNERS)), dma((2, OWNERS)),
             dma((7,)), dma((GROUP,)),
             dma((31,)), dma((OWNERS,)),
-            dma((6,)),
+            dma((9,)),
         ],
         compiler_params=pltpu.CompilerParams(
             collective_id=0, has_side_effects=True, vmem_limit_bytes=VMEM_LIMIT

time: 118 us -> 115 us (0.975)
  Pallas kernels: 117 us -> 114 us
    pallas_call x1, Pallas kernels: 115 us -> 112 us  [whole(): pl.pallas_call(whole_kernel, out_shape=(jax.ShapeDtypeStruct((ROWS, HEADS...]
where the time goes in v5:
time: 115 us
  Pallas kernels  114 us (99%)
    pallas_call x1, Pallas kernels, whole(): pl.pallas_call(whole_kernel, out_shape=(jax.ShapeDtypeStruct((ROWS, HEADS...  112 us

profile of v5, /device:TPU:1, one launch (start us, length us, event | category | flops | bytes accessed | tf_op | source)
XLA Modules:
  0.0 114.7 jit_solution(7278777240378029519)
XLA Ops:
  0.6 112.1 %attention_backward.1 = (bf16[128,1024]{1,0:T(8,128)(2,1)}, bf16[128,256]{1,0:T(8,128)(2,1)}, f32[2,32,128]{2,1,0:T(8,128)}, f32[2,32,128]{2,1,0:T(8,128)}, f32[2,32,128]{2,1,0:T(8,128)}, /*index=5*/f32[8,128]{1,0:T(8,128)}) custom-call(s32[128]{0:T(128)} %order_ref.1, bf16[128,1024]{1,0:T(8,128)(2,1)} %bitcast.7, bf16[128,1024]{1,0:T(8,128)(2,1)} %bitcast.8, ...), custom_call_target="tpu_custom_call" | custom-call | tf_op jit(solution)/shard_map/attention_backward/pallas_call | solution.py:571
  112.7 1.8 %new_weights.1 = (bf16[1,128,1024]{2,1,0:T(8,128)(2,1)}, bf16[1,128,256]{2,1,0:T(8,128)(2,1)}, f32[2,32,128]{2,1,0:T(8,128)}, f32[2,32,128]{2,1,0:T(8,128)}, f32[2,32,128]{2,1,0:T(8,128)}, /*index=5*/f32[2]{0:T(128)}) custom-call(bf16[128,1024]{1,0:T(8,128)(2,1)} %get-tuple-element.12.q_ref, bf16[128,256]{1,0:T(8,128)(2,1)} %get-tuple-element.13.kv_ref, ...), custom_call_target="tpu_custom_call" | custom-call | tf_op jit(solution)/shard_map/new_weights/pallas_call | solution.py:654

commit v6 on v5

--- a/solution.py
+++ b/solution.py
@@ -368,12 +368,12 @@
         dk_acc[...] += jnp.dot(score_grad, qg[s], preferred_element_type=F32)
         dqt[s] += jnp.dot(kt[pair], score_grad, preferred_element_type=F32)
 
-    def key_block(pair):
+    def key_block(pair, own):
         dk_acc[...] = jnp.zeros_like(dk_acc)
         dv_acc[...] = jnp.zeros_like(dv_acc)
 
         def query_step(t, carry):
-            diagonal = (t == x // 2) & (pair == rest // 2)
+            diagonal = t == x // 2
 
             @pl.when(diagonal)
             def _():
@@ -387,7 +387,11 @@
 
             return carry
 
-        lax.fori_loop(0, 2, query_step, 0)
+        if own:
+            lax.fori_loop(0, 2, query_step, 0)
+        else:
+            for s in range(8):
+                tile(pair, s, False)
         for h in range(2):
             dkv_out[2 * pair + h, 0] = dk_acc[pl.ds(h * ROWS, ROWS), :].astype(BF16)
             dkv_out[2 * pair + h, 1] = dv_acc[pl.ds(h * ROWS, ROWS), :].astype(BF16)
@@ -405,13 +409,13 @@
         )
 
     def block_step(b, carry):
-        key_block(block_of(b))
+        key_block(block_of(b), False)
         to_holder(b, 0).start()
         to_holder(b, 1).start()
         return carry
 
     lax.fori_loop(0, 7, block_step, 0)
-    key_block(rest // 2)
+    key_block(rest // 2, True)
     other = rest + 1 - 2 * (rest % 2)
     copies.append(
         send(dkv_out.at[other], dkv_in.at[rest], d_send.at[14], d_recv.at[rest],

time: 115 us -> 113 us (0.983)
    pallas_call x1, Pallas kernels: 112 us -> 111 us  [whole(): pl.pallas_call(whole_kernel, out_shape=(jax.ShapeDtypeStruct((ROWS, HEADS...]
where the time goes in v6:
time: 113 us
  Pallas kernels  113 us (100%)
    pallas_call x1, Pallas kernels, whole(): pl.pallas_call(whole_kernel, out_shape=(jax.ShapeDtypeStruct((ROWS, HEADS...  111 us

profile of v6, /device:TPU:1, one launch (start us, length us, event | category | flops | bytes accessed | tf_op | source)
XLA Modules:
  0.0 113.3 jit_solution(7241304176506555976)
XLA Ops:
  0.6 110.7 %attention_backward.1 = (bf16[128,1024]{1,0:T(8,128)(2,1)}, bf16[128,256]{1,0:T(8,128)(2,1)}, f32[2,32,128]{2,1,0:T(8,128)}, f32[2,32,128]{2,1,0:T(8,128)}, f32[2,32,128]{2,1,0:T(8,128)}, /*index=5*/f32[8,128]{1,0:T(8,128)}) custom-call(s32[128]{0:T(128)} %order_ref.1, bf16[128,1024]{1,0:T(8,128)(2,1)} %bitcast.7, bf16[128,1024]{1,0:T(8,128)(2,1)} %bitcast.8, ...), custom_call_target="tpu_custom_call" | custom-call | tf_op jit(solution)/shard_map/attention_backward/pallas_call | solution.py:575
  111.4 1.8 %new_weights.1 = (bf16[1,128,1024]{2,1,0:T(8,128)(2,1)}, bf16[1,128,256]{2,1,0:T(8,128)(2,1)}, f32[2,32,128]{2,1,0:T(8,128)}, f32[2,32,128]{2,1,0:T(8,128)}, f32[2,32,128]{2,1,0:T(8,128)}, /*index=5*/f32[2]{0:T(128)}) custom-call(bf16[128,1024]{1,0:T(8,128)(2,1)} %get-tuple-element.12.q_ref, bf16[128,256]{1,0:T(8,128)(2,1)} %get-tuple-element.13.kv_ref, ...), custom_call_target="tpu_custom_call" | custom-call | tf_op jit(solution)/shard_map/new_weights/pallas_call | solution.py:658
